TPU v7x, 512 devices: a whole 4x8x8 slice. The times are simulated.
512 devices in a mesh: inst: 16 (over y, x_hi), tp: 32 (over z, x_lo, core).
Axes of the slice: x: 4 (x_hi: 2, x_lo: 2; x = x_hi * 2 + x_lo), y: 8, z: 8, core: 2. Of those that a mesh axis runs over, the one named last changes fastest.
Arguments:
- tokens: bfloat16 [2560, 8192], P('inst'), as said below
- doc_ids: int32 [16, 160], replicated, may hold values from 0 to 3, never falling along the last dimension, each value on 1 to 80 neighbouring positions
- query_one: bfloat16 [8192, 4096], P('inst', 'tp'), as said below
- keyval_one: bfloat16 [8192, 1024], P('inst', 'tp'), as said below
- output_one: bfloat16 [4096, 8192], P('tp', 'inst'), may hold values from -0.09375 to 0.09375
- query_two: bfloat16 [8192, 4096], P('inst', 'tp'), as said below
- keyval_two: bfloat16 [8192, 1024], P('inst', 'tp'), as said below
- output_two: bfloat16 [4096, 8192], P('tp', 'inst'), may hold values from -0.1875 to 0.1875
Outputs:
- blended: bfloat16 [2560, 8192], P('inst', 'tp')
Inputs may be any that keep to these rules, and one draw needn't show every extreme that they name: `doc_ids`: along each row the document numbers never fall; each document holds 1 to 80 positions. `query_one`: A projection scaled by the square root of its fan-in. `keyval_one`: A projection scaled by the square root of its fan-in. `query_two`: A projection scaled by the square root of its fan-in. `keyval_two`: A projection scaled by the square root of its fan-in. `tokens`: hidden rows of order one.
All inputs are finite; a program needn't handle non-finite values.
Results may differ from a plain program's by a relative error of at most 0.034.
Values may be sent and summed in bfloat16 or wider, within the bound.
A program may use at most 64 MiB of HBM per device.

v0:
```python
import jax
import jax.numpy as jnp
from jax import lax
from jax.sharding import PartitionSpec as P

GROUP = 8


def from_partner(block, axis, bit):
    count = lax.axis_size(axis)
    route = []
    for low in range(count):
        high = low | 1 << bit
        if high != low and high < count:
            route += [(low, high), (high, low)]
    return lax.ppermute(block, axis, route)


def passed_along(block, axis, distance):
    devices = range(lax.axis_size(axis))
    route = [((i - distance) % len(devices), i) for i in devices]
    return lax.ppermute(block, axis, route)


def normalize(hidden):
    floats = hidden.astype(jnp.float32)
    scale = lax.rsqrt(jnp.mean(floats * floats, axis=1, keepdims=True) + 1e-06)
    return (floats * scale).astype(jnp.bfloat16)


def share_head(own_piece):
    gathered = own_piece
    group_rank = lax.axis_index("tp")
    for bit_level in range(GROUP.bit_length() - 1):
        partner = from_partner(gathered, "tp", bit_level)
        is_lower = group_rank // 2**bit_level % 2 == 0
        gathered = jnp.where(
            is_lower,
            jnp.concatenate([gathered, partner], 1),
            jnp.concatenate([partner, gathered], 1),
        )
    return gathered


def head_terms(hidden, doc_row, query_shard, keyval_shard, output_shard):
    normed = normalize(hidden)
    row_count = normed.shape[0]
    query_total = jnp.dot(
        normed,
        lax.all_gather(query_shard, "inst", axis=0, tiled=True),
        preferred_element_type=jnp.float32,
    )
    keyval_total = jnp.dot(
        normed,
        lax.all_gather(keyval_shard, "inst", axis=0, tiled=True),
        preferred_element_type=jnp.float32,
    )
    head_dim = query_shard.shape[1]
    queries = (query_total * head_dim ** (-0.5)).astype(jnp.bfloat16)
    keyvals = share_head(keyval_total.astype(jnp.bfloat16))
    key_rows = keyvals[:, :head_dim]
    value_rows = keyvals[:, head_dim:]
    scores = lax.dot_general(
        queries, key_rows, (((1,), (1,)), ((), ())), preferred_element_type=jnp.float32
    )
    position = jnp.arange(row_count)
    allowed = (doc_row[:, None] == doc_row[None, :]) & (position[None, :] <= position[:, None])
    scores = jnp.where(allowed, scores, -1e30)
    row_top = jnp.max(scores, axis=1, keepdims=True)
    weights = jnp.exp(scores - row_top)
    probabilities = (weights / jnp.sum(weights, axis=1, keepdims=True)).astype(jnp.bfloat16)
    context = jnp.dot(probabilities, value_rows, preferred_element_type=jnp.float32).astype(
        jnp.bfloat16
    )
    return jnp.dot(
        context,
        lax.all_gather(output_shard, "inst", axis=1, tiled=True),
        preferred_element_type=jnp.float32,
    )


def shards(tokens, doc_ids, query_one, keyval_one, output_one, query_two, keyval_two, output_two):
    inst_count = lax.axis_size("inst")
    inst_place = lax.axis_index("inst")
    own_docs = lax.dynamic_index_in_dim(doc_ids, inst_place, 0, keepdims=False)
    prev_docs = lax.dynamic_index_in_dim(
        doc_ids, (inst_place + inst_count - 1) % inst_count, 0, keepdims=False
    )
    first_terms = head_terms(tokens, own_docs, query_one, keyval_one, output_one)
    column_width = tokens.shape[1] // lax.axis_size("tp")
    tensor_rank = lax.axis_index("tp")
    summed = lax.psum(first_terms.astype(jnp.bfloat16), "tp").astype(jnp.float32)
    middle = (tokens.astype(jnp.float32) + summed).astype(jnp.bfloat16)
    arrived = passed_along(middle, "inst", 1)
    second_terms = head_terms(arrived, prev_docs, query_two, keyval_two, output_two)
    shares = lax.psum_scatter(
        second_terms.astype(jnp.bfloat16), "tp", scatter_dimension=1, tiled=True
    ).astype(jnp.float32)
    residual_part = lax.dynamic_slice_in_dim(arrived, tensor_rank * column_width, column_width, 1)
    return (residual_part.astype(jnp.float32) + shares).astype(jnp.bfloat16)


def solution(mesh):
    placed = (
        P("inst", None),
        P(),
        P("inst", "tp"),
        P("inst", "tp"),
        P("tp", "inst"),
        P("inst", "tp"),
        P("inst", "tp"),
        P("tp", "inst"),
    )
    return jax.shard_map(
        shards, mesh=mesh, in_specs=placed, out_specs=P("inst", "tp"), check_vma=False
    )
```

profile of v0, /device:TPU:24, one launch (start us, length us, event | category | flops | bytes accessed | tf_op | source)
XLA Modules:
  0.0 767.3 jit_solution(14264077675794599022)
XLA Ops:
  8.1 2.4 fusion.2
  10.4 40.9 %all_gather.19 = bf16[8192,32]{0,1:T(8,128)(2,1)S(1)} all-gather(bf16[512,32]{0,1:T(8,128)(2,1)S(1)} %copy-done.1), channel_id=1, replica_groups=mesh['inst'=16,'tp'=32] {'inst'}, dimensions={0}, use_global_device_ids=true | all-gather | bytes 557056 | tf_op jit(solution)/shard_map/all_gather | solution.py:55
  52.3 1.9 collective-permute-start
  55.4 2.6 collective-permute-start.1
  58.0 3.2 collective-permute-done.1
  61.2 4.5 collective-permute-start.2
  68.1 37.4 %all-gather.5.cloned.1.call-done = bf16[8192,128]{1,0:T(8,128)(2,1)} async-done(((bf16[512,128]{1,0:T(8,128)(2,1)}), bf16[8192,128]{1,0:T(8,128)(2,1)}) %all-gather.5.cloned.1.call-update) | async-done | bytes 2097168 | tf_op jit(solution)/shard_map/all_gather | solution.py:50
  105.4 2.7 fusion.35
  108.2 87.1 %all-gather.7.cloned.1.call-done = bf16[128,8192]{1,0:T(8,128)(2,1)} async-done(((bf16[128,512]{1,0:T(8,128)(2,1)}), bf16[128,8192]{1,0:T(8,128)(2,1)}) %all-gather.7.cloned.1.call-update) | async-done | bytes 2097168 | tf_op jit(solution)/shard_map/all_gather | solution.py:77
  195.3 4.1 convolution_convert_fusion.1
  200.1 236.2 %all-reduce.2.cloned.1.call-done = bf16[160,8192]{1,0:T(8,128)(2,1)} async-done(((bf16[160,8192]{1,0:T(8,128)(2,1)}), bf16[160,8192]{1,0:T(8,128)(2,1)}) %all-reduce.2.cloned.1.call-update) | async-done | bytes 2621456 | tf_op jit(solution)/shard_map/psum | solution.py:92
  436.3 4.1 fusion.4
  440.3 4.7 collective-permute-start.3
  445.1 99.5 %all_gather.22 = bf16[8192,32]{0,1:T(8,128)(2,1)S(1)} all-gather(bf16[512,32]{0,1:T(8,128)(2,1)S(1)} %copy-done.2), channel_id=1, replica_groups=mesh['inst'=16,'tp'=32] {'inst'}, dimensions={0}, use_global_device_ids=true | all-gather | bytes 557056 | tf_op jit(solution)/shard_map/all_gather | solution.py:55
  546.2 1.9 collective-permute-start.4
  549.3 1.9 collective-permute-start.5
  551.3 3.9 collective-permute-done.5
  555.2 1.9 collective-permute-start.6
  557.1 4.2 collective-permute-done.6
  561.4 2.7 fusion.38
  564.1 69.2 %all-gather.11.cloned.1.call-done = bf16[128,8192]{1,0:T(8,128)(2,1)} async-done(((bf16[128,512]{1,0:T(8,128)(2,1)}), bf16[128,8192]{1,0:T(8,128)(2,1)}) %all-gather.11.cloned.1.call-update) | async-done | bytes 2097168 | tf_op jit(solution)/shard_map/all_gather | solution.py:77
  633.3 4.2 convolution_convert_fusion
  637.5 121.4 %reduce-scatter.2.cloned.1.call-done = bf16[160,256]{1,0:T(8,128)(2,1)} async-done(((bf16[160,8192]{1,0:T(8,128)(2,1)}), bf16[160,256]{1,0:T(8,128)(2,1)}) %reduce-scatter.2.cloned.1.call-update) | async-done | bytes 81936 | tf_op jit(solution)/shard_map/reduce_scatter | solution.py:96
  758.9 1.5 add_convert_fusion
  (37 shorter events, 9.6 us)
Async XLA Ops:
  6.5 44.8 %copy-start = (bf16[160,8192]{1,0:T(8,128)(2,1)S(1)}, bf16[160,8192]{1,0:T(8,128)(2,1)}, u32[]{:S(2)}) copy-start(bf16[160,8192]{1,0:T(8,128)(2,1)} %param.8) | copy-start | bytes 7864324
  6.5 3.9 copy-start.1
  6.5 98.9 %all-gather.5.cloned.1.call-start = ((), (), s32[]{:S(2)}) async-start(), calls=%async_computation.1 | async-start | bytes 2228224 | tf_op jit(solution)/shard_map/all_gather | solution.py:50
  7.3 188.0 %all-gather.7.cloned.1.call-start = ((), (), s32[]{:S(2)}) async-start(), calls=%async_computation.2 | async-start | bytes 2228224 | tf_op jit(solution)/shard_map/all_gather | solution.py:77
  8.0 428.2 %all-reduce.2.cloned.1.call-start = ((), (), s32[]{:S(2)}) async-start(), calls=%async_computation.3 | async-start | bytes 5242880 | tf_op jit(solution)/shard_map/psum | solution.py:92
  52.3 3.1 collective-permute-start
  55.4 5.8 collective-permute-start.1
  61.2 6.8 collective-permute-start.2
  199.4 361.9 %all-gather.9.cloned.1.call-start = ((), (), s32[]{:S(2)}) async-start(), calls=%async_computation.4 | async-start | bytes 2228224 | tf_op jit(solution)/shard_map/all_gather | solution.py:50
  200.0 245.1 %copy-start.2 = (bf16[512,32]{0,1:T(8,128)(2,1)S(1)}, bf16[512,32]{0,1:T(8,128)(2,1)}, u32[]{:S(2)}) copy-start(bf16[512,32]{0,1:T(8,128)(2,1)} %param.14) | copy-start | bytes 98308
  200.0 433.3 %all-gather.11.cloned.1.call-start = ((), (), s32[]{:S(2)}) async-start(), calls=%async_computation.5 | async-start | bytes 2228224 | tf_op jit(solution)/shard_map/all_gather | solution.py:77
  440.3 104.2 %collective-permute-start.3 = (bf16[160,8192]{1,0:T(8,128)(2,1)}, bf16[160,8192]{1,0:T(8,128)(2,1)S(1)}, u32[]{:S(2)}, u32[]{:S(2)}) collective-permute-start(bf16[160,8192]{1,0:T(8,128)(2,1)} %fusion.4), channel_id=1, source_target_pairs={{480,0},{0,32},{32,64},{64,96},{96,128},{128,160},{160,192},{192,2... | collective-permute-start | bytes 7864328 | tf_op jit(solution)/shard_map/ppermute | solution.py:22
  445.0 313.9 %reduce-scatter.2.cloned.1.call-start = ((), (), s32[]{:S(2)}) async-start(), calls=%async_computation.6 | async-start | bytes 2703360 | tf_op jit(solution)/shard_map/reduce_scatter | solution.py:96
  546.2 3.1 collective-permute-start.4
  549.3 5.8 collective-permute-start.5
  555.2 6.2 collective-permute-start.6
Sparse Core Ops, SparseCore 0:
  10.5 94.8 all-gather.4
  108.5 86.7 all-gather.6
  199.5 236.6 all-reduce.1
  439.3 108.0 all-gather.8
  550.3 82.9 all-gather.10
  637.6 121.2 reduce-scatter.1
where the time goes:
time: 768 us; the launch traced here: 767 us
  waiting for transfers between devices  568 us (74%)
  blocking collectives  140 us (18%)
  starting transfers between devices  19.7 us (3%)
  matrix products  15.7 us (2%)
  between operations  13.7 us (2%)
  other arithmetic  8.83 us (1%)
    psum x1, waiting for transfers between devices, shards(): lax.psum(first_terms.astype(jnp.bfloat16), 'tp').astype(jnp.float32)  236 us
    all_gather x2, waiting for transfers between devices, head_terms(): lax.all_gather(output_shard, 'inst', axis=1, tiled=True)  156 us
    all_gather x2, blocking collectives, head_terms(): lax.all_gather(keyval_shard, 'inst', axis=0, tiled=True)  140 us
    reduce_scatter x1, waiting for transfers between devices, shards(): lax.psum_scatter(second_terms.astype(jnp.bfloat16), 'tp', scatter_dimensi...  121 us
    all_gather x2, waiting for transfers between devices, head_terms(): lax.all_gather(query_shard, 'inst', axis=0, tiled=True)  37.4 us
  transfers between devices with their start and end apart: 13, of which 11 were waited for; matrix products, arithmetic and copies ran while one was open for 2% of the time, Pallas kernels for 0%

commit v1 on v0

v1 whole, which is shorter than its diff:
```python
import functools

import jax
import jax.numpy as jnp
from jax import lax
from jax.experimental import pallas as pl
from jax.experimental.pallas import tpu as pltpu
from jax.sharding import PartitionSpec as P

MESH = pl.DeviceIdType.MESH
F32 = jnp.float32
BF16 = jnp.bfloat16
NT = (((1,), (1,)), ((), ()))
ROWS = 160
HEAD = 128
PIECE = 32
WIDE = 256
GROUP = 8
REACH = ((4, 3), (3, 4))


def dot_nt(left, right):
    return lax.dot_general(left, right, NT, preferred_element_type=F32)


def kernel(
    ny,
    nz,
    tokens,
    docs,
    query_one,
    keyval_one,
    output_one,
    query_two,
    keyval_two,
    output_two,
    out,
    wq,
    wkv,
    wo,
    kvin,
    kvt,
    docs_in,
    mask,
    xs,
    aq,
    akv,
    ass,
    near_s,
    near_r,
    far_s,
    far_r,
    tail_pad,
    kvs,
    ctx,
    pbuf,
    rs_s,
    rs_r,
    half_s,
    half_r,
    fin,
    local_sem,
    xlocal_sem,
    swap_ss,
    swap_rs,
    y_ss,
    y_rs,
    tok_ss,
    tok_rs,
    near_ss,
    near_rs,
    far_ss,
    far_rs,
    kv_ss,
    kv_rs,
    ctx_ss,
    ctx_rs,
    z_ss,
    z_rs,
    half_ss,
    half_rs,
    ag_ss,
    ag_rs,
    one_ss,
    one_rs,
):
    inst = lax.axis_index("inst")
    rank = lax.axis_index("tp")
    ninst, nrank = 2 * ny, 4 * nz
    y, x_hi = inst // 2, inst % 2
    z, x_lo, c = rank // 4, rank // 2 % 2, rank % 2
    piece = rank % GROUP
    model = ny * 2 * 512

    mate = (inst, rank + 1 - 2 * c)
    across = (inst + 1 - 2 * x_hi, rank)
    across_mate = (inst + 1 - 2 * x_hi, rank + 1 - 2 * c)
    beside = (inst, rank + 2 - 4 * x_lo)
    y_next = (((inst + 2) % ninst, rank), ((inst + ninst - 2) % ninst, rank))
    z_next = ((inst, (rank + 4) % nrank), (inst, (rank + nrank - 4) % nrank))
    goal = ((2 * y + x_lo + 1) % ninst, 4 * z + 2 * x_hi + c)
    origin_inst = (inst + ninst - 1) % ninst
    origin = (origin_inst // 2 * 2 + rank // 2 % 2, 4 * z + 2 * (1 - x_hi) + c)

    group_base = rank // GROUP * GROUP
    sharers = [(inst, group_base + (piece + o) % GROUP) for o in range(1, GROUP)]
    other_z = (inst, (rank + nrank + 4 * (2 * (z % 2) - 1)) % nrank)

    barrier = pltpu.get_barrier_semaphore()
    greeted = sharers + [other_z, y_next[0], y_next[1], across, across_mate, origin]
    for peer in greeted:
        pl.semaphore_signal(barrier, inc=1, device_id=peer, device_id_type=MESH)

    sent = []

    def copy(src, dst, send, recv, peer):
        return pltpu.make_async_remote_copy(
            src_ref=src,
            dst_ref=dst,
            send_sem=send,
            recv_sem=recv,
            device_id=peer,
            device_id_type=MESH,
        )

    def send(*args):
        move = copy(*args)
        move.start()
        sent.append(move)

    def landed(dst, send_sem, recv_sem):
        copy(dst, dst, send_sem, recv_sem, mate).wait_recv()

    queries = (query_one, query_two)
    keyvals = (keyval_one, keyval_two)
    outputs = (output_one, output_two)
    loads = {}

    def load(name, src, dst, sem):
        loads[name] = pltpu.make_async_copy(src, dst, sem)
        loads[name].start()

    def quarter(block, hi):
        return pl.ds(pl.multiple_of((2 * block + hi) * 512 + c * WIDE, WIDE), WIDE)

    own_k = pl.ds(pl.multiple_of(c * WIDE, WIDE), WIDE)
    mate_k = pl.ds(pl.multiple_of((1 - c) * WIDE, WIDE), WIDE)
    load("kv0", keyvals[0], kvin.at[0], local_sem.at[0])
    load("q0", queries[0].at[own_k, :], wq.at[0, y, c], local_sem.at[1])
    for b in range(nz):
        load(("x", b), tokens.at[:, quarter(b, x_hi)], xs.at[0, b, x_hi], xlocal_sem.at[b])
    load("o0", outputs[0].at[:, own_k], wo.at[0, y, c], local_sem.at[2])
    load("docs", docs, docs_in, local_sem.at[3])
    load("kv1", keyvals[1], kvin.at[1], local_sem.at[4])
    load("q1", queries[1].at[own_k, :], wq.at[1, y, c], local_sem.at[5])
    load("o1", outputs[1].at[:, own_k], wo.at[1, y, c], local_sem.at[6])

    pl.semaphore_wait(barrier, len(greeted))

    def swap(n, src, dst):
        send(src, dst, swap_ss.at[n], swap_rs.at[n], mate)

    def swapped(n, dst):
        landed(dst, swap_ss.at[n], swap_rs.at[n])

    swap(0, queries[0].at[mate_k, :], wq.at[0, y, c])
    send(tokens.at[:, quarter(z, 1 - x_hi)], xs.at[0, z, x_hi], one_ss.at[0], one_rs.at[0], across)

    eye = (
        lax.broadcasted_iota(jnp.int32, (PIECE, PIECE), 0)
        == lax.broadcasted_iota(jnp.int32, (PIECE, PIECE), 1)
    ).astype(BF16)

    def turn_keyvals(layer):
        loads[f"kv{layer}"].wait()
        for half in range(2):
            kvt[layer, half] = dot_nt(eye, kvin[layer, half * WIDE : (half + 1) * WIDE, :]).astype(BF16)
        wkv[layer, y, c] = kvt[layer, c]
        swap(4 + layer, kvt.at[layer, 1 - c], wkv.at[layer, y, c])

    def ring_step(step, slot, me, n, peers, reach, ss, rs):
        for way in range(2):
            sign = 1 if way == 0 else n - 1
            block = (me + (n - sign) * (step - 1)) % n
            if 1 < step <= reach[way] + 1:
                landed(slot(block), ss.at[way, step - 2], rs.at[way, step - 2])
            if step <= reach[way]:
                ref = slot(block)
                send(ref, ref, ss.at[way, step - 1], rs.at[way, step - 1], peers[way])

    def query_step(layer, step):
        if step == 1:
            loads[f"q{layer}"].wait()
        for lane in range(2):
            head = c if lane == 0 else 1 - c
            if step == 1 and lane == 1:
                swapped(2 * layer, wq.at[layer, y, 1 - c])
            unit = 5 * layer + lane
            ring_step(step, lambda b: wq.at[layer, b, head], y, ny, y_next, REACH[lane], y_ss.at[unit], y_rs.at[unit])
        if step == 1:
            swapped(4 + layer, wkv.at[layer, y, 1 - c])
        unit = 5 * layer + 2
        ring_step(step, lambda b: wkv.at[layer, b], y, ny, y_next, REACH[layer], y_ss.at[unit], y_rs.at[unit])

    def output_step(layer, step):
        if step == 1:
            loads[f"o{layer}"].wait()
        for lane in range(2):
            head = c if lane == 0 else 1 - c
            if step == 1 and lane == 1:
                swapped(2 * layer + 1, wo.at[layer, y, 1 - c])
            unit = 5 * layer + 3 + lane
            ring_step(step, lambda b: wo.at[layer, b, head], y, ny, y_next, REACH[lane], y_ss.at[unit], y_rs.at[unit])

    def token_step(step):
        if step == 1:
            landed(xs.at[0, z, 1 - x_hi], one_ss.at[0], one_rs.at[0])
        ring_step(step, lambda b: xs.at[0, b, 1 - x_hi], z, nz, z_next, REACH[0], tok_ss, tok_rs)

    turn_keyvals(0)
    swap(1, outputs[0].at[:, mate_k], wo.at[0, y, c])
    query_step(0, 1)
    token_step(1)
    swap(2, queries[1].at[mate_k, :], wq.at[1, y, c])
    swap(3, outputs[1].at[:, mate_k], wo.at[1, y, c])
    turn_keyvals(1)

    loads["docs"].wait()
    doc_row = jnp.broadcast_to(docs_in[pl.ds(inst, 1), :], (ROWS, ROWS)).astype(F32)
    place_t = lax.broadcasted_iota(jnp.int32, (ROWS, ROWS), 0)
    place_s = lax.broadcasted_iota(jnp.int32, (ROWS, ROWS), 1)
    doc_col = dot_nt((place_t == place_s).astype(BF16), doc_row.astype(BF16))
    allowed = (doc_col == doc_row) & (place_s <= place_t)
    mask[...] = jnp.zeros_like(mask)
    mask[:, :ROWS] = jnp.where(allowed, 1.0, 0.0)
    tail_pad[...] = jnp.zeros_like(tail_pad)

    for b in range(nz):
        loads[("x", b)].wait()
    for step in range(2, 6):
        query_step(0, step)
        token_step(step)
    output_step(0, 1)

    lane_at = lax.broadcasted_iota(jnp.int32, (ROWS, HEAD), 1)
    select = (
        lax.broadcasted_iota(jnp.int32, (PIECE, HEAD), 0)
        == lax.broadcasted_iota(jnp.int32, (PIECE, HEAD), 1)
    ).astype(BF16)

    def pack(ref, q, tail, squares):
        high = squares.astype(BF16).astype(F32)
        low = squares - high
        tail = jnp.where(lane_at < PIECE, tail, jnp.where(lane_at == PIECE, high, 0.0))
        tail = jnp.where(lane_at == PIECE + 1, low, tail)
        ref[:, :HEAD] = q.astype(BF16)
        ref[:, HEAD:] = tail.astype(BF16)

    def squares_of(tail):
        return jnp.sum(jnp.where(lane_at < PIECE, 0.0, tail), axis=1, keepdims=True)

    def project(layer, first, last):
        def body(b, carry):
            x = xs[layer, b].reshape(2 * ROWS, WIDE)
            w = jnp.concatenate([wq[layer, b, 0], wq[layer, b, 1]], axis=1)
            q = jnp.dot(x, w, preferred_element_type=F32).reshape(2, ROWS, WIDE)
            xf = x.astype(F32)
            sq = (xf[:, :HEAD] * xf[:, :HEAD] + xf[:, HEAD:] * xf[:, HEAD:]).reshape(2, ROWS, HEAD)
            ass[...] += sq
            for h in range(2):
                aq[h] += q[:, :, h * HEAD : (h + 1) * HEAD]
                akv[h, :, :, :PIECE] += dot_nt(x, wkv[layer, b, h]).reshape(2, ROWS, PIECE)
            return carry

        lax.fori_loop(first, last, body, 0)

    def heads(layer, beside_step):
        aq[...] = jnp.zeros_like(aq)
        akv[...] = jnp.zeros_like(akv)
        ass[...] = jnp.zeros_like(ass)
        project(layer, 0, nz)
        for k in (1 - x_hi, x_hi):
            squares = jnp.sum(ass[k], axis=1, keepdims=True)
            pack(near_s.at[layer, k], aq[1 - c, k], akv[1 - c, k], squares)
            send(near_s.at[layer, k], near_r.at[layer, k], near_ss.at[layer, k], near_rs.at[layer, k], mate)
        beside_step(2)

        def chip_sum(k):
            landed(near_r.at[layer, k], near_ss.at[layer, k], near_rs.at[layer, k])
            squares = jnp.sum(ass[k], axis=1, keepdims=True)
            other = near_r[layer, k].astype(F32)
            tail = jnp.where(lane_at < PIECE, akv[c, k], jnp.where(lane_at == PIECE, squares, 0.0))
            return aq[c, k] + other[:, :HEAD], tail + other[:, HEAD:]

        q, tail = chip_sum(1 - x_hi)
        pack(far_s.at[layer], q, tail, squares_of(tail))
        send(far_s.at[layer], far_r.at[layer], far_ss.at[layer], far_rs.at[layer], across)
        beside_step(3)
        q, tail = chip_sum(x_hi)
        landed(far_r.at[layer], far_ss.at[layer], far_rs.at[layer])
        other = far_r[layer].astype(F32)
        q = q + other[:, :HEAD]
        tail = tail + other[:, HEAD:]
        scale = lax.rsqrt(squares_of(tail) * (1.0 / model) + 1e-06)
        q = (q * scale * HEAD**-0.5).astype(BF16)
        tail_pad[:ROWS, :] = jnp.where(lane_at < PIECE, tail * scale, 0.0).astype(BF16)
        kvs[layer, piece] = dot_nt(select, tail_pad[...]).astype(BF16)
        for n, peer in enumerate(sharers):
            ref = kvs.at[layer, piece]
            send(ref, ref, kv_ss.at[layer, n], kv_rs.at[layer, piece], peer)
        beside_step(4)
        for o in range(1, GROUP):
            p = (piece + o) % GROUP
            landed(kvs.at[layer, p], kv_ss.at[layer, 0], kv_rs.at[layer, p])
        keys = kvs[layer, 0:4].reshape(HEAD, WIDE)
        values = kvs[layer, 4:8].reshape(HEAD, WIDE)
        scores = jnp.dot(q, keys, preferred_element_type=F32)
        scores = jnp.where(mask[...] > 0.5, scores, -1e30)
        top = jnp.max(scores, axis=1, keepdims=True)
        weights = jnp.exp(scores - top)
        probs = (weights / jnp.sum(weights, axis=1, keepdims=True)).astype(BF16)
        ctx[layer, x_hi, c] = dot_nt(probs, values).astype(BF16)
        ref = ctx.at[layer, x_hi, c]
        slot = 2 * x_hi + c
        for n, peer in enumerate((across, across_mate, mate)):
            send(ref, ref, ctx_ss.at[layer, n], ctx_rs.at[layer, slot], peer)
        beside_step(5)
        for other_slot in (2 * x_hi + 1 - c, 2 * (1 - x_hi) + c, 2 * (1 - x_hi) + 1 - c):
            landed(ctx.at[layer, other_slot // 2, other_slot % 2], ctx_ss.at[layer, 0], ctx_rs.at[layer, other_slot])

    def reduce(layer, beside_step):
        ks = (1 - x_lo, x_lo)

        def product(b):
            left = jnp.concatenate([ctx[layer, :, 0].reshape(2 * ROWS, HEAD), ctx[layer, :, 1].reshape(2 * ROWS, HEAD)], axis=1)
            right = wo[layer, b].reshape(2 * HEAD, WIDE)
            pbuf[b] = jnp.dot(left, right, preferred_element_type=F32).reshape(2, ROWS, WIDE)

        def hop(lane, way, distance):
            b = (z + (distance if way == 0 else nz - distance)) % nz
            value = pbuf[b, ks[lane]]
            if distance < REACH[lane][way]:
                landed(rs_r.at[layer, lane, way, distance], z_ss.at[layer, lane, way, distance], z_rs.at[layer, lane, way, distance])
                value = value + rs_r[layer, lane, way, distance].astype(F32)
            if distance == 0:
                return value
            rs_s[layer, lane, way, distance - 1] = value.astype(BF16)
            send(
                rs_s.at[layer, lane, way, distance - 1],
                rs_r.at[layer, lane, way, distance - 1],
                z_ss.at[layer, lane, way, distance - 1],
                z_rs.at[layer, lane, way, distance - 1],
                z_next[way],
            )

        product((z + 4) % nz)
        hop(0, 0, 4)
        hop(1, 1, 4)

        def rest(j, carry):
            product((z + 5 + j) % nz)
            return carry

        lax.fori_loop(0, nz - 1, rest, 0)
        hop(1, 0, 3)
        hop(0, 1, 3)
        beside_step(1)
        hop(0, 0, 3)
        hop(1, 1, 3)
        for distance in (2, 1):
            hop(1, 0, distance)
            hop(0, 1, distance)
            hop(0, 0, distance)
            hop(1, 1, distance)
            beside_step(4 - distance)

        def collected(lane):
            total = hop(lane, 0, 0)
            landed(rs_r.at[layer, lane, 1, 0], z_ss.at[layer, lane, 1, 0], z_rs.at[layer, lane, 1, 0])
            return total + rs_r[layer, lane, 1, 0].astype(F32)

        half_s[layer] = collected(0).astype(BF16)
        send(half_s.at[layer], half_r.at[layer], half_ss.at[layer], half_rs.at[layer], beside)
        mine = collected(1)
        beside_step(4)
        landed(half_r.at[layer], half_ss.at[layer], half_rs.at[layer])
        mine = mine + half_r[layer].astype(F32)
        return (xs[layer, z, x_lo].astype(F32) + mine).astype(BF16)

    def nothing(step):
        pass

    heads(0, lambda step: output_step(0, step))
    middle = reduce(0, lambda step: query_step(1, step))
    xs[1, z, x_lo] = middle
    ref = xs.at[1, z, x_lo]
    send(ref, ref, one_ss.at[1], one_rs.at[1], beside)
    query_step(1, 5)
    for step in range(1, 6):
        for lane in range(2):
            k = x_lo if lane == 0 else 1 - x_lo
            if step == 1 and lane == 1:
                landed(xs.at[1, z, k], one_ss.at[1], one_rs.at[1])
            ring_step(step, lambda b: xs.at[1, b, k], z, nz, z_next, REACH[lane], ag_ss.at[lane], ag_rs.at[lane])
        output_step(1, step)
    heads(1, nothing)
    fin[...] = reduce(1, nothing)
    send(fin, out, one_ss.at[2], one_rs.at[2], goal)
    for move in sent:
        move.wait_send()
    landed(out, one_ss.at[2], one_rs.at[2])


def solution(mesh):
    ny, nz = mesh.shape["inst"] // 2, mesh.shape["tp"] // 4

    def shards(*operands):
        dma = pltpu.SemaphoreType.DMA
        anywhere = pl.BlockSpec(memory_space=pl.ANY)
        vmem = pltpu.VMEM
        return pl.pallas_call(
            functools.partial(kernel, ny, nz),
            out_shape=jax.ShapeDtypeStruct((ROWS, WIDE), BF16),
            in_specs=[anywhere] * 8,
            out_specs=anywhere,
            scratch_shapes=[
                vmem((2, ny, 2, WIDE, HEAD), BF16),
                vmem((2, ny, 2, PIECE, WIDE), BF16),
                vmem((2, ny, 2, HEAD, WIDE), BF16),
                vmem((2, 2 * WIDE, PIECE), BF16),
                vmem((2, 2, PIECE, WIDE), BF16),
                vmem((2 * ny, ROWS), jnp.int32),
                vmem((ROWS, WIDE), F32),
                vmem((2, nz, 2, ROWS, WIDE), BF16),
                vmem((2, 2, ROWS, HEAD), F32),
                vmem((2, 2, ROWS, HEAD), F32),
                vmem((2, ROWS, HEAD), F32),
                vmem((2, 2, ROWS, WIDE), BF16),
                vmem((2, 2, ROWS, WIDE), BF16),
                vmem((2, ROWS, WIDE), BF16),
                vmem((2, ROWS, WIDE), BF16),
                vmem((WIDE, HEAD), BF16),
                vmem((2, GROUP, PIECE, WIDE), BF16),
                vmem((2, 2, 2, ROWS, HEAD), BF16),
                vmem((nz, 2, ROWS, WIDE), F32),
                vmem((2, 2, 2, 4, ROWS, WIDE), BF16),
                vmem((2, 2, 2, 4, ROWS, WIDE), BF16),
                vmem((2, ROWS, WIDE), BF16),
                vmem((2, ROWS, WIDE), BF16),
                vmem((ROWS, WIDE), BF16),
                dma((7,)),
                dma((nz,)),
                dma((6,)),
                dma((6,)),
                dma((10, 2, 4)),
                dma((10, 2, 4)),
                dma((2, 4)),
                dma((2, 4)),
                dma((2, 2)),
                dma((2, 2)),
                dma((2,)),
                dma((2,)),
                dma((2, GROUP)),
                dma((2, GROUP)),
                dma((2, 3)),
                dma((2, 4)),
                dma((2, 2, 2, 4)),
                dma((2, 2, 2, 4)),
                dma((2,)),
                dma((2,)),
                dma((2, 2, 4)),
                dma((2, 2, 4)),
                dma((3,)),
                dma((3,)),
            ],
            compiler_params=pltpu.CompilerParams(
                collective_id=0,
                has_side_effects=True,
                vmem_limit_bytes=40 * 1024 * 1024,
            ),
            cost_estimate=pl.CostEstimate(
                flops=2_000_000_000, bytes_accessed=10_000_000, transcendentals=51200
            ),
        )(*operands)

    placed = (
        P("inst", None),
        P(),
        P("inst", "tp"),
        P("inst", "tp"),
        P("tp", "inst"),
        P("inst", "tp"),
        P("inst", "tp"),
        P("tp", "inst"),
    )
    return jax.shard_map(
        shards, mesh=mesh, in_specs=placed, out_specs=P("inst", "tp"), check_vma=False
    )
```

time: 768 us -> 144 us (0.19)
  the two profiles are of different devices: /device:TPU:24 before, /device:TPU:2 now
where the time goes in v1:
time: 144 us; the launch traced here: 143 us
  Pallas kernels  135 us (94%)
  local copies, waits for them, and re-layouts  8.47 us (6%)
    pallas_call x1, Pallas kernels, shards(): pl.pallas_call(functools.partial(kernel, ny, nz), out_shape=jax.ShapeDtyp...  135 us
    unnamed x15, local copies, waits for them, and re-layouts  8.47 us

profile of v1, /device:TPU:2, one launch (start us, length us, event | category | flops | bytes accessed | tf_op | source)
XLA Modules:
  0.0 143.2 jit_solution(9700823603186701797)
XLA Ops:
  0.0 0.9 copy.9.keyval_one
  0.9 0.9 copy.10.keyval_two
  1.8 0.0 copy-start
  1.8 1.7 %copy-done = bf16[160,8192]{1,0:T(8,128)(2,1)S(1)} copy-done((bf16[160,8192]{1,0:T(8,128)(2,1)S(1)}, bf16[160,8192]{1,0:T(8,128)(2,1)}, u32[]{:S(2)}) %copy-start) | copy-done | bytes 2621464
  3.5 0.0 copy-start.1
  3.5 0.9 copy-done.1
  4.4 0.0 copy-start.2
  4.4 0.9 copy-done.2
  5.3 0.0 copy-start.3
  5.3 0.9 copy-done.3
  6.2 0.0 copy-start.4
  6.2 0.9 copy-done.4
  7.1 0.0 copy-start.5
  7.1 0.7 copy-done.5
  7.8 134.7 %shard_map.82 = bf16[160,256]{1,0:T(8,128)(2,1)S(1)} custom-call(bf16[160,8192]{1,0:T(8,128)(2,1)S(1)} %copy-done, s32[16,160]{1,0:T(8,128)S(1)} %copy-done.5, bf16[512,128]{1,0:T(8,128)(2,1)S(1)} %copy-done.1, bf16[512,32]{1,0:T(8,128)(2,1)S(1)} %copy.9.keyval_one, bf16[128,512]{1,0:T(8,128)(2,1)S(1)} %copy-done.2, bf16[512,128]{1,0:T(8,128)(2,1)S(1)} %copy-done.3, ...), custom_call_target="tpu_custom_call" | custom-call | flops 2000000000 | bytes 10000000 | tf_op jit(solution)/shard_map/pallas_call | solution.py:421
  142.5 0.6 copy.12
Async XLA Ops:
  1.8 1.7 %copy-start = (bf16[160,8192]{1,0:T(8,128)(2,1)S(1)}, bf16[160,8192]{1,0:T(8,128)(2,1)}, u32[]{:S(2)}) copy-start(bf16[160,8192]{1,0:T(8,128)(2,1)} %tokens.1) | copy-start | bytes 7864324
  3.5 0.9 copy-start.1
  4.4 0.9 copy-start.2
  5.3 0.9 copy-start.3
  6.2 0.9 copy-start.4
  7.1 0.7 copy-start.5

commit v2 on v1

--- a/solution.py
+++ b/solution.py
@@ -38,11 +38,10 @@
     wq,
     wkv,
     wo,
-    kvin,
-    kvt,
     docs_in,
     mask,
     xs,
+    xs_two,
     aq,
     akv,
     ass,
@@ -56,8 +55,6 @@
     pbuf,
     rs_s,
     rs_r,
-    half_s,
-    half_r,
     fin,
     local_sem,
     xlocal_sem,
@@ -77,12 +74,12 @@
     ctx_rs,
     z_ss,
     z_rs,
-    half_ss,
-    half_rs,
     ag_ss,
     ag_rs,
     one_ss,
     one_rs,
+    fin_ss,
+    fin_rs,
 ):
     inst = lax.axis_index("inst")
     rank = lax.axis_index("tp")
@@ -94,22 +91,27 @@
 
     mate = (inst, rank + 1 - 2 * c)
     across = (inst + 1 - 2 * x_hi, rank)
-    across_mate = (inst + 1 - 2 * x_hi, rank + 1 - 2 * c)
     beside = (inst, rank + 2 - 4 * x_lo)
     y_next = (((inst + 2) % ninst, rank), ((inst + ninst - 2) % ninst, rank))
     z_next = ((inst, (rank + 4) % nrank), (inst, (rank + nrank - 4) % nrank))
-    goal = ((2 * y + x_lo + 1) % ninst, 4 * z + 2 * x_hi + c)
-    origin_inst = (inst + ninst - 1) % ninst
-    origin = (origin_inst // 2 * 2 + rank // 2 % 2, 4 * z + 2 * (1 - x_hi) + c)
+    beside_mate = (inst, rank + 3 - 4 * x_lo - 2 * c)
+    goals = [((2 * y + k + 1) % ninst, 4 * z + 2 * x_hi + c) for k in range(2)]
+    origin_inst = (inst + ninst - 1) % ninst // 2 * 2 + x_lo
+    origins = [(origin_inst, 4 * z + 2 * s + c) for s in range(2)]
+    stays = x_hi * x_lo
 
     group_base = rank // GROUP * GROUP
     sharers = [(inst, group_base + (piece + o) % GROUP) for o in range(1, GROUP)]
     other_z = (inst, (rank + nrank + 4 * (2 * (z % 2) - 1)) % nrank)
 
     barrier = pltpu.get_barrier_semaphore()
-    greeted = sharers + [other_z, y_next[0], y_next[1], across, across_mate, origin]
+    greeted = sharers + [other_z, y_next[0], y_next[1], across, origins[0]]
     for peer in greeted:
         pl.semaphore_signal(barrier, inc=1, device_id=peer, device_id_type=MESH)
+
+    @pl.when(stays == 0)
+    def _():
+        pl.semaphore_signal(barrier, inc=1, device_id=origins[1], device_id_type=MESH)
 
     sent = []
 
@@ -145,38 +147,40 @@
 
     own_k = pl.ds(pl.multiple_of(c * WIDE, WIDE), WIDE)
     mate_k = pl.ds(pl.multiple_of((1 - c) * WIDE, WIDE), WIDE)
-    load("kv0", keyvals[0], kvin.at[0], local_sem.at[0])
+    own_part = pl.ds(pl.multiple_of((2 * c + x_lo) * HEAD, HEAD), HEAD)
+    load("kv0", keyvals[0].at[:, own_k], wkv.at[0, y, c], local_sem.at[0])
     load("q0", queries[0].at[own_k, :], wq.at[0, y, c], local_sem.at[1])
     for b in range(nz):
-        load(("x", b), tokens.at[:, quarter(b, x_hi)], xs.at[0, b, x_hi], xlocal_sem.at[b])
-    load("o0", outputs[0].at[:, own_k], wo.at[0, y, c], local_sem.at[2])
+        load(("x", b), tokens.at[:, quarter(b, x_hi)], xs.at[b, x_hi], xlocal_sem.at[b])
+    load("o0", outputs[0].at[:, own_part], wo.at[0, y, x_lo, c], local_sem.at[2])
     load("docs", docs, docs_in, local_sem.at[3])
-    load("kv1", keyvals[1], kvin.at[1], local_sem.at[4])
+    load("kv1", keyvals[1].at[:, own_k], wkv.at[1, y, c], local_sem.at[4])
     load("q1", queries[1].at[own_k, :], wq.at[1, y, c], local_sem.at[5])
-    load("o1", outputs[1].at[:, own_k], wo.at[1, y, c], local_sem.at[6])
-
-    pl.semaphore_wait(barrier, len(greeted))
-
-    def swap(n, src, dst):
-        send(src, dst, swap_ss.at[n], swap_rs.at[n], mate)
-
-    def swapped(n, dst):
-        landed(dst, swap_ss.at[n], swap_rs.at[n])
-
-    swap(0, queries[0].at[mate_k, :], wq.at[0, y, c])
-    send(tokens.at[:, quarter(z, 1 - x_hi)], xs.at[0, z, x_hi], one_ss.at[0], one_rs.at[0], across)
-
-    eye = (
-        lax.broadcasted_iota(jnp.int32, (PIECE, PIECE), 0)
-        == lax.broadcasted_iota(jnp.int32, (PIECE, PIECE), 1)
-    ).astype(BF16)
-
-    def turn_keyvals(layer):
-        loads[f"kv{layer}"].wait()
-        for half in range(2):
-            kvt[layer, half] = dot_nt(eye, kvin[layer, half * WIDE : (half + 1) * WIDE, :]).astype(BF16)
-        wkv[layer, y, c] = kvt[layer, c]
-        swap(4 + layer, kvt.at[layer, 1 - c], wkv.at[layer, y, c])
+    load("o1", outputs[1].at[:, own_part], wo.at[1, y, x_lo, c], local_sem.at[6])
+
+    pl.semaphore_wait(barrier, len(greeted) + 1 - stays)
+
+    def swap(layer, n, src, dst, peer):
+        send(src, dst, swap_ss.at[layer, n], swap_rs.at[layer, n], peer)
+
+    def swapped(layer, n, dst):
+        landed(dst, swap_ss.at[layer, n], swap_rs.at[layer, n])
+
+    def swap_query(layer):
+        swap(layer, 0, queries[layer].at[mate_k, :], wq.at[layer, y, c], mate)
+        swap(layer, 1, keyvals[layer].at[:, mate_k], wkv.at[layer, y, c], mate)
+
+    def part(lo, core):
+        return pl.ds(pl.multiple_of((2 * core + lo) * HEAD, HEAD), HEAD)
+
+    def swap_output(layer):
+        dst = wo.at[layer, y, x_lo, c]
+        swap(layer, 2, outputs[layer].at[:, part(x_lo, 1 - c)], dst, mate)
+        swap(layer, 3, outputs[layer].at[:, part(1 - x_lo, c)], dst, beside)
+        swap(layer, 4, outputs[layer].at[:, part(1 - x_lo, 1 - c)], dst, beside_mate)
+
+    swap_query(0)
+    send(tokens.at[:, quarter(z, 1 - x_hi)], xs.at[z, x_hi], one_ss.at[0], one_rs.at[0], across)
 
     def ring_step(step, slot, me, n, peers, reach, ss, rs):
         for way in range(2):
@@ -194,11 +198,12 @@
         for lane in range(2):
             head = c if lane == 0 else 1 - c
             if step == 1 and lane == 1:
-                swapped(2 * layer, wq.at[layer, y, 1 - c])
+                swapped(layer, 0, wq.at[layer, y, 1 - c])
             unit = 5 * layer + lane
             ring_step(step, lambda b: wq.at[layer, b, head], y, ny, y_next, REACH[lane], y_ss.at[unit], y_rs.at[unit])
         if step == 1:
-            swapped(4 + layer, wkv.at[layer, y, 1 - c])
+            loads[f"kv{layer}"].wait()
+            swapped(layer, 1, wkv.at[layer, y, 1 - c])
         unit = 5 * layer + 2
         ring_step(step, lambda b: wkv.at[layer, b], y, ny, y_next, REACH[layer], y_ss.at[unit], y_rs.at[unit])
 
@@ -206,24 +211,25 @@
         if step == 1:
             loads[f"o{layer}"].wait()
         for lane in range(2):
-            head = c if lane == 0 else 1 - c
+            lo = x_lo if lane == 0 else 1 - x_lo
+            if step == 1 and lane == 0:
+                swapped(layer, 2, wo.at[layer, y, x_lo, 1 - c])
             if step == 1 and lane == 1:
-                swapped(2 * layer + 1, wo.at[layer, y, 1 - c])
+                swapped(layer, 3, wo.at[layer, y, 1 - x_lo, c])
+                swapped(layer, 4, wo.at[layer, y, 1 - x_lo, 1 - c])
             unit = 5 * layer + 3 + lane
-            ring_step(step, lambda b: wo.at[layer, b, head], y, ny, y_next, REACH[lane], y_ss.at[unit], y_rs.at[unit])
+            ring_step(step, lambda b: wo.at[layer, b, lo], y, ny, y_next, REACH[lane], y_ss.at[unit], y_rs.at[unit])
 
     def token_step(step):
         if step == 1:
-            landed(xs.at[0, z, 1 - x_hi], one_ss.at[0], one_rs.at[0])
-        ring_step(step, lambda b: xs.at[0, b, 1 - x_hi], z, nz, z_next, REACH[0], tok_ss, tok_rs)
-
-    turn_keyvals(0)
-    swap(1, outputs[0].at[:, mate_k], wo.at[0, y, c])
+            landed(xs.at[z, 1 - x_hi], one_ss.at[0], one_rs.at[0])
+        ring_step(step, lambda b: xs.at[b, 1 - x_hi], z, nz, z_next, REACH[0], tok_ss, tok_rs)
+
     query_step(0, 1)
+    swap_output(0)
     token_step(1)
-    swap(2, queries[1].at[mate_k, :], wq.at[1, y, c])
-    swap(3, outputs[1].at[:, mate_k], wo.at[1, y, c])
-    turn_keyvals(1)
+    swap_query(1)
+    swap_output(1)
 
     loads["docs"].wait()
     doc_row = jnp.broadcast_to(docs_in[pl.ds(inst, 1), :], (ROWS, ROWS)).astype(F32)
@@ -235,13 +241,6 @@
     mask[:, :ROWS] = jnp.where(allowed, 1.0, 0.0)
     tail_pad[...] = jnp.zeros_like(tail_pad)
 
-    for b in range(nz):
-        loads[("x", b)].wait()
-    for step in range(2, 6):
-        query_step(0, step)
-        token_step(step)
-    output_step(0, 1)
-
     lane_at = lax.broadcasted_iota(jnp.int32, (ROWS, HEAD), 1)
     select = (
         lax.broadcasted_iota(jnp.int32, (PIECE, HEAD), 0)
@@ -259,9 +258,18 @@
     def squares_of(tail):
         return jnp.sum(jnp.where(lane_at < PIECE, 0.0, tail), axis=1, keepdims=True)
 
-    def project(layer, first, last):
-        def body(b, carry):
-            x = xs[layer, b].reshape(2 * ROWS, WIDE)
+    def clear():
+        aq[...] = jnp.zeros_like(aq)
+        akv[...] = jnp.zeros_like(akv)
+        ass[...] = jnp.zeros_like(ass)
+
+    def project(layer, first, count):
+        def body(j, carry):
+            b = (first + j) % nz
+            if layer == 0:
+                x = xs[b].reshape(2 * ROWS, WIDE)
+            else:
+                x = jnp.concatenate([xs_two[b, 0].reshape(2 * ROWS, HEAD), xs_two[b, 1].reshape(2 * ROWS, HEAD)], axis=1)
             w = jnp.concatenate([wq[layer, b, 0], wq[layer, b, 1]], axis=1)
             q = jnp.dot(x, w, preferred_element_type=F32).reshape(2, ROWS, WIDE)
             xf = x.astype(F32)
@@ -272,13 +280,9 @@
                 akv[h, :, :, :PIECE] += dot_nt(x, wkv[layer, b, h]).reshape(2, ROWS, PIECE)
             return carry
 
-        lax.fori_loop(first, last, body, 0)
+        lax.fori_loop(0, count, body, 0)
 
     def heads(layer, beside_step):
-        aq[...] = jnp.zeros_like(aq)
-        akv[...] = jnp.zeros_like(akv)
-        ass[...] = jnp.zeros_like(ass)
-        project(layer, 0, nz)
         for k in (1 - x_hi, x_hi):
             squares = jnp.sum(ass[k], axis=1, keepdims=True)
             pack(near_s.at[layer, k], aq[1 - c, k], akv[1 - c, k], squares)
@@ -319,22 +323,33 @@
         top = jnp.max(scores, axis=1, keepdims=True)
         weights = jnp.exp(scores - top)
         probs = (weights / jnp.sum(weights, axis=1, keepdims=True)).astype(BF16)
-        ctx[layer, x_hi, c] = dot_nt(probs, values).astype(BF16)
-        ref = ctx.at[layer, x_hi, c]
-        slot = 2 * x_hi + c
-        for n, peer in enumerate((across, across_mate, mate)):
-            send(ref, ref, ctx_ss.at[layer, n], ctx_rs.at[layer, slot], peer)
+        place = 2 * x_lo + c
+        ctx[layer, x_hi, place] = dot_nt(probs, values).astype(BF16)
+        spread(layer, x_hi, (across, mate, beside, beside_mate), 0)
         beside_step(5)
-        for other_slot in (2 * x_hi + 1 - c, 2 * (1 - x_hi) + c, 2 * (1 - x_hi) + 1 - c):
-            landed(ctx.at[layer, other_slot // 2, other_slot % 2], ctx_ss.at[layer, 0], ctx_rs.at[layer, other_slot])
+
+    def spread(layer, k, peers, first):
+        ref = ctx.at[layer, k, 2 * x_lo + c]
+        for n, peer in enumerate(peers):
+            send(ref, ref, ctx_ss.at[layer, first + n], ctx_rs.at[layer, k, 2 * x_lo + c], peer)
+
+    def spread_in(layer, k, place):
+        landed(ctx.at[layer, k, place], ctx_ss.at[layer, 0], ctx_rs.at[layer, k, place])
 
     def reduce(layer, beside_step):
-        ks = (1 - x_lo, x_lo)
-
-        def product(b):
-            left = jnp.concatenate([ctx[layer, :, 0].reshape(2 * ROWS, HEAD), ctx[layer, :, 1].reshape(2 * ROWS, HEAD)], axis=1)
-            right = wo[layer, b].reshape(2 * HEAD, WIDE)
-            pbuf[b] = jnp.dot(left, right, preferred_element_type=F32).reshape(2, ROWS, WIDE)
+        ks = (x_hi, 1 - x_hi)
+        others = (2 * x_lo + 1 - c, 2 * (1 - x_lo) + c, 2 * (1 - x_lo) + 1 - c)
+
+        def products(k):
+            left = jnp.concatenate([ctx[layer, k, n] for n in range(4)], axis=1)
+
+            def body(j, carry):
+                b = (z + 4 + j) % nz
+                right = wo[layer, b].reshape(4 * HEAD, HEAD)
+                pbuf[b, k] = jnp.dot(left, right, preferred_element_type=F32)
+                return carry
+
+            lax.fori_loop(0, nz, body, 0)
 
         def hop(lane, way, distance):
             b = (z + (distance if way == 0 else nz - distance)) % nz
@@ -353,70 +368,122 @@
                 z_next[way],
             )
 
-        product((z + 4) % nz)
+        spread_in(layer, 1 - x_hi, 2 * x_lo + c)
+        spread(layer, 1 - x_hi, (mate, beside, beside_mate), 4)
+        for place in others:
+            spread_in(layer, x_hi, place)
+        products(x_hi)
         hop(0, 0, 4)
-        hop(1, 1, 4)
-
-        def rest(j, carry):
-            product((z + 5 + j) % nz)
-            return carry
-
-        lax.fori_loop(0, nz - 1, rest, 0)
-        hop(1, 0, 3)
         hop(0, 1, 3)
         beside_step(1)
+        for place in others:
+            spread_in(layer, 1 - x_hi, place)
+        products(1 - x_hi)
+        hop(1, 1, 4)
+        hop(1, 0, 3)
         hop(0, 0, 3)
+        hop(0, 1, 2)
+        beside_step(2)
         hop(1, 1, 3)
-        for distance in (2, 1):
-            hop(1, 0, distance)
-            hop(0, 1, distance)
-            hop(0, 0, distance)
-            hop(1, 1, distance)
-            beside_step(4 - distance)
+        hop(1, 0, 2)
+        hop(0, 0, 2)
+        hop(0, 1, 1)
+        beside_step(3)
+        hop(1, 1, 2)
+        hop(1, 0, 1)
+        hop(0, 0, 1)
+        beside_step(4)
+        hop(1, 1, 1)
 
         def collected(lane):
             total = hop(lane, 0, 0)
             landed(rs_r.at[layer, lane, 1, 0], z_ss.at[layer, lane, 1, 0], z_rs.at[layer, lane, 1, 0])
-            return total + rs_r[layer, lane, 1, 0].astype(F32)
-
-        half_s[layer] = collected(0).astype(BF16)
-        send(half_s.at[layer], half_r.at[layer], half_ss.at[layer], half_rs.at[layer], beside)
-        mine = collected(1)
-        beside_step(4)
-        landed(half_r.at[layer], half_ss.at[layer], half_rs.at[layer])
-        mine = mine + half_r[layer].astype(F32)
-        return (xs[layer, z, x_lo].astype(F32) + mine).astype(BF16)
+            total = total + rs_r[layer, lane, 1, 0].astype(F32)
+            k = ks[lane]
+            if layer == 0:
+                old = xs[z, k, :, pl.ds(pl.multiple_of(x_lo * HEAD, HEAD), HEAD)]
+            else:
+                old = xs_two[z, x_lo, k]
+            return (old.astype(F32) + total).astype(BF16)
+
+        return collected
 
     def nothing(step):
         pass
 
+    clear()
+    for b in range(nz):
+        loads[("x", b)].wait()
+    query_step(0, 2)
+    token_step(2)
+    query_step(0, 3)
+    token_step(3)
+    token_step(4)
+    query_step(0, 4)
+    token_step(5)
+    output_step(0, 1)
+    project(0, y + ny - 3, ny - 1)
+    query_step(0, 5)
+    project(0, y + 4, 1)
     heads(0, lambda step: output_step(0, step))
-    middle = reduce(0, lambda step: query_step(1, step))
-    xs[1, z, x_lo] = middle
-    ref = xs.at[1, z, x_lo]
+    collected = reduce(0, lambda step: query_step(1, step))
+    for lane in range(2):
+        k = x_hi if lane == 0 else 1 - x_hi
+        xs_two[z, x_lo, k] = collected(lane)
+    ref = xs_two.at[z, x_lo]
     send(ref, ref, one_ss.at[1], one_rs.at[1], beside)
-    query_step(1, 5)
     for step in range(1, 6):
         for lane in range(2):
-            k = x_lo if lane == 0 else 1 - x_lo
+            half = x_lo if lane == 0 else 1 - x_lo
             if step == 1 and lane == 1:
-                landed(xs.at[1, z, k], one_ss.at[1], one_rs.at[1])
-            ring_step(step, lambda b: xs.at[1, b, k], z, nz, z_next, REACH[lane], ag_ss.at[lane], ag_rs.at[lane])
+                landed(xs_two.at[z, half], one_ss.at[1], one_rs.at[1])
+            ring_step(step, lambda b: xs_two.at[b, half], z, nz, z_next, REACH[lane], ag_ss.at[lane], ag_rs.at[lane])
+        if step == 1:
+            query_step(1, 5)
+            clear()
         output_step(1, step)
+        if step == 4:
+            project(1, z + nz - 3, nz - 1)
+    project(1, z + 4, 1)
     heads(1, nothing)
-    fin[...] = reduce(1, nothing)
-    send(fin, out, one_ss.at[2], one_rs.at[2], goal)
+    collected = reduce(1, nothing)
+    for lane in range(2):
+        k = x_hi if lane == 0 else 1 - x_hi
+        fin[k] = collected(lane)
+    own_half = pl.ds(pl.multiple_of(x_lo * HEAD, HEAD), HEAD)
+    moves = [
+        copy(fin.at[k], out.at[:, own_half], fin_ss.at[k], fin_rs.at[x_lo], goals[k]) for k in range(2)
+    ]
+    moves[1].start()
+
+    @pl.when(stays == 0)
+    def _():
+        moves[0].start()
+        moves[0].wait_send()
+
+    @pl.when(stays == 1)
+    def _():
+        keep = pltpu.make_async_copy(fin.at[0], out.at[:, own_half], local_sem.at[0])
+        keep.start()
+        keep.wait()
+
+    moves[1].wait_send()
     for move in sent:
         move.wait_send()
-    landed(out, one_ss.at[2], one_rs.at[2])
+    landed(out.at[:, :HEAD], fin_ss.at[0], fin_rs.at[0])
+
+    @pl.when(stays == 0)
+    def _():
+        landed(out.at[:, HEAD:], fin_ss.at[1], fin_rs.at[1])
 
 
 def solution(mesh):
     ny, nz = mesh.shape["inst"] // 2, mesh.shape["tp"] // 4
 
-    def shards(*operands):
+    def shards(tokens, docs, q1, kv1, o1, q2, kv2, o2):
+        operands = [pltpu.with_memory_space_constraint(a, pltpu.HBM) for a in (tokens, docs, q1, kv1.T, o1, q2, kv2.T, o2)]
         dma = pltpu.SemaphoreType.DMA
-        anywhere = pl.BlockSpec(memory_space=pl.ANY)
+        anywhere = pl.BlockSpec(memory_space=pltpu.HBM)
         vmem = pltpu.VMEM
         return pl.pallas_call(
             functools.partial(kernel, ny, nz),
@@ -426,12 +493,11 @@
             scratch_shapes=[
                 vmem((2, ny, 2, WIDE, HEAD), BF16),
                 vmem((2, ny, 2, PIECE, WIDE), BF16),
-                vmem((2, ny, 2, HEAD, WIDE), BF16),
-                vmem((2, 2 * WIDE, PIECE), BF16),
-                vmem((2, 2, PIECE, WIDE), BF16),
+                vmem((2, ny, 2, 2, HEAD, HEAD), BF16),
                 vmem((2 * ny, ROWS), jnp.int32),
                 vmem((ROWS, WIDE), F32),
-                vmem((2, nz, 2, ROWS, WIDE), BF16),
+                vmem((nz, 2, ROWS, WIDE), BF16),
+                vmem((nz, 2, 2, ROWS, HEAD), BF16),
                 vmem((2, 2, ROWS, HEAD), F32),
                 vmem((2, 2, ROWS, HEAD), F32),
                 vmem((2, ROWS, HEAD), F32),
@@ -441,17 +507,15 @@
                 vmem((2, ROWS, WIDE), BF16),
                 vmem((WIDE, HEAD), BF16),
                 vmem((2, GROUP, PIECE, WIDE), BF16),
-                vmem((2, 2, 2, ROWS, HEAD), BF16),
-                vmem((nz, 2, ROWS, WIDE), F32),
-                vmem((2, 2, 2, 4, ROWS, WIDE), BF16),
-                vmem((2, 2, 2, 4, ROWS, WIDE), BF16),
-                vmem((2, ROWS, WIDE), BF16),
-                vmem((2, ROWS, WIDE), BF16),
-                vmem((ROWS, WIDE), BF16),
+                vmem((2, 2, 4, ROWS, HEAD), BF16),
+                vmem((nz, 2, ROWS, HEAD), F32),
+                vmem((2, 2, 2, 4, ROWS, HEAD), BF16),
+                vmem((2, 2, 2, 4, ROWS, HEAD), BF16),
+                vmem((2, ROWS, HEAD), BF16),
                 dma((7,)),
                 dma((nz,)),
-                dma((6,)),
-                dma((6,)),
+                dma((2, 5)),
+                dma((2, 5)),
                 dma((10, 2, 4)),
                 dma((10, 2, 4)),
                 dma((2, 4)),
@@ -462,16 +526,16 @@
                 dma((2,)),
                 dma((2, GROUP)),
                 dma((2, GROUP)),
-                dma((2, 3)),
-                dma((2, 4)),
+                dma((2, 7)),
+                dma((2, 2, 4)),
                 dma((2, 2, 2, 4)),
                 dma((2, 2, 2, 4)),
+                dma((2, 2, 4)),
+                dma((2, 2, 4)),
                 dma((2,)),
                 dma((2,)),
-                dma((2, 2, 4)),
-                dma((2, 2, 4)),
-                dma((3,)),
-                dma((3,)),
+                dma((2,)),
+                dma((2,)),
             ],
             compiler_params=pltpu.CompilerParams(
                 collective_id=0,

time: 144 us -> 132 us (0.917)
  local copies, waits for them, and re-layouts: 8.47 us -> 0.64 us
  Pallas kernels: 135 us -> 131 us
    unnamed x15 -> x1, local copies, waits for them, and re-layouts: 8.47 us -> 0.64 us
    pallas_call x1, Pallas kernels: 135 us -> 131 us  [shards(): pl.pallas_call(functools.partial(kernel, ny, nz), out_shape=jax.ShapeDtyp...]
where the time goes in v2:
time: 132 us
  Pallas kernels  131 us (99%)
    pallas_call x1, Pallas kernels, shards(): pl.pallas_call(functools.partial(kernel, ny, nz), out_shape=jax.ShapeDtyp...  131 us

profile of v2, /device:TPU:2, one launch (start us, length us, event | category | flops | bytes accessed | tf_op | source)
XLA Modules:
  0.0 131.7 jit_solution(10978577086275513829)
XLA Ops:
  0.0 131.1 %shard_map.82 = bf16[160,256]{1,0:T(8,128)(2,1)S(1)} custom-call(bf16[160,8192]{1,0:T(8,128)(2,1)} %tokens.1, s32[16,160]{1,0:T(8,128)} %docs.1, bf16[512,128]{1,0:T(8,128)(2,1)} %query_one.1, bf16[32,512]{1,0:T(8,128)(2,1)} %bitcast.2, bf16[128,512]{1,0:T(8,128)(2,1)} %output_one.1, bf16[512,128]{1,0:T(8,128)(2,1)} %query_two.1, bf16[32,512]{1,0:T(8,128)(2,1)} %bitcast.3, ...), custom_call_target="tpu_custom_call" | custom-call | flops 2000000000 | bytes 10000000 | tf_op jit(solution)/shard_map/pallas_call | solution.py:488
  131.1 0.6 copy.10

commit v3 on v2

--- a/solution.py
+++ b/solution.py
@@ -94,6 +94,8 @@
     beside = (inst, rank + 2 - 4 * x_lo)
     y_next = (((inst + 2) % ninst, rank), ((inst + ninst - 2) % ninst, rank))
     z_next = ((inst, (rank + 4) % nrank), (inst, (rank + nrank - 4) % nrank))
+    across_beside = (inst + 1 - 2 * x_hi, rank + 2 - 4 * x_lo)
+    across_beside_mate = (inst + 1 - 2 * x_hi, rank + 3 - 4 * x_lo - 2 * c)
     beside_mate = (inst, rank + 3 - 4 * x_lo - 2 * c)
     goals = [((2 * y + k + 1) % ninst, 4 * z + 2 * x_hi + c) for k in range(2)]
     origin_inst = (inst + ninst - 1) % ninst // 2 * 2 + x_lo
@@ -102,10 +104,15 @@
 
     group_base = rank // GROUP * GROUP
     sharers = [(inst, group_base + (piece + o) % GROUP) for o in range(1, GROUP)]
-    other_z = (inst, (rank + nrank + 4 * (2 * (z % 2) - 1)) % nrank)
+    other_rank = (rank + nrank + 4 * (2 * (z % 2) - 1)) % nrank
+    other_z = (inst, other_rank)
+    other_diagonal = (inst, other_rank + 2 - 4 * x_lo)
+    z_second = ((inst, (rank + 8) % nrank), (inst, (rank + nrank - 8) % nrank))
+    diagonal = tuple((inst, peer + 2 - 4 * x_lo) for _, peer in z_next)
 
     barrier = pltpu.get_barrier_semaphore()
-    greeted = sharers + [other_z, y_next[0], y_next[1], across, origins[0]]
+    greeted = sharers + [other_z, other_diagonal, *z_second, *y_next, across, origins[0]]
+    greeted += [across_beside, across_beside_mate]
     for peer in greeted:
         pl.semaphore_signal(barrier, inc=1, device_id=peer, device_id_type=MESH)
 
@@ -180,54 +187,108 @@
         swap(layer, 4, outputs[layer].at[:, part(1 - x_lo, 1 - c)], dst, beside_mate)
 
     swap_query(0)
-    send(tokens.at[:, quarter(z, 1 - x_hi)], xs.at[z, x_hi], one_ss.at[0], one_rs.at[0], across)
-
-    def ring_step(step, slot, me, n, peers, reach, ss, rs):
+    token_rows = [pl.ds(lane * (ROWS // 2), ROWS // 2) for lane in range(2)]
+    for lane, rows in enumerate(token_rows):
+        src = tokens.at[rows, quarter(z, 1 - x_hi)]
+        send(src, xs.at[z, x_hi, rows], one_ss.at[3 * lane], one_rs.at[3 * lane], across_beside)
+
+    def ring_step(step, slot, me, n, peers, reach, ss, rs, opens=True):
         for way in range(2):
             sign = 1 if way == 0 else n - 1
             block = (me + (n - sign) * (step - 1)) % n
             if 1 < step <= reach[way] + 1:
                 landed(slot(block), ss.at[way, step - 2], rs.at[way, step - 2])
-            if step <= reach[way]:
+            if step <= reach[way] and (opens or step > 1):
                 ref = slot(block)
                 send(ref, ref, ss.at[way, step - 1], rs.at[way, step - 1], peers[way])
 
     def query_step(layer, step):
         if step == 1:
             loads[f"q{layer}"].wait()
-        for lane in range(2):
-            head = c if lane == 0 else 1 - c
-            if step == 1 and lane == 1:
+        for lane in range(4):
+            head = c if lane < 2 else 1 - c
+            if step == 1 and lane == 2:
                 swapped(layer, 0, wq.at[layer, y, 1 - c])
-            unit = 5 * layer + lane
-            ring_step(step, lambda b: wq.at[layer, b, head], y, ny, y_next, REACH[lane], y_ss.at[unit], y_rs.at[unit])
+            unit = 9 * layer + lane
+            rows = pl.ds(lane % 2 * HEAD, HEAD)
+            ring_step(
+                step,
+                lambda b: wq.at[layer, b, head, rows],
+                y,
+                ny,
+                y_next,
+                REACH[lane % 2],
+                y_ss.at[unit],
+                y_rs.at[unit],
+            )
         if step == 1:
             loads[f"kv{layer}"].wait()
             swapped(layer, 1, wkv.at[layer, y, 1 - c])
-        unit = 5 * layer + 2
+        unit = 9 * layer + 4
         ring_step(step, lambda b: wkv.at[layer, b], y, ny, y_next, REACH[layer], y_ss.at[unit], y_rs.at[unit])
 
     def output_step(layer, step):
         if step == 1:
             loads[f"o{layer}"].wait()
+        for lane in range(4):
+            lo = x_lo if lane < 2 else 1 - x_lo
+            core = c if lane % 2 == 0 else 1 - c
+            if step == 1 and lane > 0:
+                swapped(layer, 1 + lane, wo.at[layer, y, lo, core])
+            unit = 9 * layer + 5 + lane
+            ring_step(
+                step,
+                lambda b: wo.at[layer, b, lo, core],
+                y,
+                ny,
+                y_next,
+                REACH[lane % 2],
+                y_ss.at[unit],
+                y_rs.at[unit],
+            )
+
+    def token_part(b, lane):
+        return xs.at[b, 1 - x_hi, token_rows[lane]]
+
+    def token_block(way, distance):
+        return (z + (nz - distance if way == 0 else distance)) % nz
+
+    def token_send(lane, way, message, b, peers):
+        ref = token_part(b, lane)
+        send(ref, ref, tok_ss.at[lane, way, message], tok_rs.at[lane, way, message], peers[way])
+
+    def token_landed(lane, way, distance):
+        n = distance - 1
+        landed(token_part(token_block(way, distance), lane), tok_ss.at[lane, way, n], tok_rs.at[lane, way, n])
+
+    def token_open():
         for lane in range(2):
-            lo = x_lo if lane == 0 else 1 - x_lo
-            if step == 1 and lane == 0:
-                swapped(layer, 2, wo.at[layer, y, x_lo, 1 - c])
-            if step == 1 and lane == 1:
-                swapped(layer, 3, wo.at[layer, y, 1 - x_lo, c])
-                swapped(layer, 4, wo.at[layer, y, 1 - x_lo, 1 - c])
-            unit = 5 * layer + 3 + lane
-            ring_step(step, lambda b: wo.at[layer, b, lo], y, ny, y_next, REACH[lane], y_ss.at[unit], y_rs.at[unit])
-
-    def token_step(step):
-        if step == 1:
-            landed(xs.at[z, 1 - x_hi], one_ss.at[0], one_rs.at[0])
-        ring_step(step, lambda b: xs.at[b, 1 - x_hi], z, nz, z_next, REACH[0], tok_ss, tok_rs)
+            landed(token_part(z, lane), one_ss.at[3 * lane], one_rs.at[3 * lane])
+            for way in range(2):
+                token_send(lane, way, 1, z, z_second)
+            for way in range(2):
+                token_send(lane, way, 0, z, z_next)
+
+    def token_forward():
+        for lane in range(2):
+            for way in range(2):
+                token_landed(lane, way, 2)
+                b = token_block(way, 2)
+                if way == lane:
+                    token_send(lane, way, 3, b, z_second)
+                token_send(lane, way, 2, b, z_next)
+
+    def token_close():
+        for lane in range(2):
+            for way in range(2):
+                token_landed(lane, way, 1)
+                token_landed(lane, way, 3)
+                if way == lane:
+                    token_landed(lane, way, 4)
 
     query_step(0, 1)
     swap_output(0)
-    token_step(1)
+    token_open()
     swap_query(1)
     swap_output(1)
 
@@ -325,7 +386,8 @@
         probs = (weights / jnp.sum(weights, axis=1, keepdims=True)).astype(BF16)
         place = 2 * x_lo + c
         ctx[layer, x_hi, place] = dot_nt(probs, values).astype(BF16)
-        spread(layer, x_hi, (across, mate, beside, beside_mate), 0)
+        peers = (across, across_beside, across_beside_mate, beside, beside_mate, mate)
+        spread(layer, x_hi, peers, 0)
         beside_step(5)
 
     def spread(layer, k, peers, first):
@@ -340,65 +402,73 @@
         ks = (x_hi, 1 - x_hi)
         others = (2 * x_lo + 1 - c, 2 * (1 - x_lo) + c, 2 * (1 - x_lo) + 1 - c)
 
-        def products(k):
+        def products(k, first, last):
             left = jnp.concatenate([ctx[layer, k, n] for n in range(4)], axis=1)
 
             def body(j, carry):
-                b = (z + 4 + j) % nz
+                b = (z + 3 + j) % nz
                 right = wo[layer, b].reshape(4 * HEAD, HEAD)
                 pbuf[b, k] = jnp.dot(left, right, preferred_element_type=F32)
                 return carry
 
-            lax.fori_loop(0, nz, body, 0)
-
-        def hop(lane, way, distance):
-            b = (z + (distance if way == 0 else nz - distance)) % nz
-            value = pbuf[b, ks[lane]]
-            if distance < REACH[lane][way]:
-                landed(rs_r.at[layer, lane, way, distance], z_ss.at[layer, lane, way, distance], z_rs.at[layer, lane, way, distance])
-                value = value + rs_r[layer, lane, way, distance].astype(F32)
-            if distance == 0:
-                return value
-            rs_s[layer, lane, way, distance - 1] = value.astype(BF16)
+            lax.fori_loop(first, last, body, 0)
+
+        def block(way, distance):
+            return (z + (distance if way == 0 else nz - distance)) % nz
+
+        def put(lane, way, message, value, peers):
+            rs_s[layer, lane, way, message] = value.astype(BF16)
             send(
-                rs_s.at[layer, lane, way, distance - 1],
-                rs_r.at[layer, lane, way, distance - 1],
-                z_ss.at[layer, lane, way, distance - 1],
-                z_rs.at[layer, lane, way, distance - 1],
-                z_next[way],
+                rs_s.at[layer, lane, way, message],
+                rs_r.at[layer, lane, way, message],
+                z_ss.at[layer, lane, way, message],
+                z_rs.at[layer, lane, way, message],
+                peers[way],
             )
 
-        spread_in(layer, 1 - x_hi, 2 * x_lo + c)
-        spread(layer, 1 - x_hi, (mate, beside, beside_mate), 4)
+        def got(lane, way, message):
+            landed(
+                rs_r.at[layer, lane, way, message],
+                z_ss.at[layer, lane, way, message],
+                z_rs.at[layer, lane, way, message],
+            )
+            return rs_r[layer, lane, way, message].astype(F32)
+
+        def set_out(lane):
+            k = ks[lane]
+            products(k, 0, 3)
+            put(lane, lane, 0, pbuf[block(lane, 4), k], z_second)
+            for way in range(2):
+                put(lane, way, 1, pbuf[block(way, 3), k], z_next)
+            products(k, 3, nz)
+            for way in range(2):
+                put(lane, way, 3, pbuf[block(way, 1), k], z_next)
+
+        def pass_on(lane):
+            for way in range(2):
+                value = pbuf[block(way, 2), ks[lane]] + got(lane, way, 1)
+                if way == lane:
+                    value = value + got(lane, way, 0)
+                put(lane, way, 2, value, z_second)
+
+        beside_step(1)
         for place in others:
             spread_in(layer, x_hi, place)
-        products(x_hi)
-        hop(0, 0, 4)
-        hop(0, 1, 3)
-        beside_step(1)
+        spread_in(layer, 1 - x_hi, 2 * x_lo + c)
+        spread(layer, 1 - x_hi, (mate,), 6)
+        set_out(0)
         for place in others:
             spread_in(layer, 1 - x_hi, place)
-        products(1 - x_hi)
-        hop(1, 1, 4)
-        hop(1, 0, 3)
-        hop(0, 0, 3)
-        hop(0, 1, 2)
+        set_out(1)
         beside_step(2)
-        hop(1, 1, 3)
-        hop(1, 0, 2)
-        hop(0, 0, 2)
-        hop(0, 1, 1)
+        pass_on(0)
+        pass_on(1)
         beside_step(3)
-        hop(1, 1, 2)
-        hop(1, 0, 1)
-        hop(0, 0, 1)
-        beside_step(4)
-        hop(1, 1, 1)
 
         def collected(lane):
-            total = hop(lane, 0, 0)
-            landed(rs_r.at[layer, lane, 1, 0], z_ss.at[layer, lane, 1, 0], z_rs.at[layer, lane, 1, 0])
-            total = total + rs_r[layer, lane, 1, 0].astype(F32)
+            total = pbuf[z, ks[lane]]
+            for way in range(2):
+                total = total + got(lane, way, 3) + got(lane, way, 2)
             k = ks[lane]
             if layer == 0:
                 old = xs[z, k, :, pl.ds(pl.multiple_of(x_lo * HEAD, HEAD), HEAD)]
@@ -415,37 +485,54 @@
     for b in range(nz):
         loads[("x", b)].wait()
     query_step(0, 2)
-    token_step(2)
+    token_forward()
     query_step(0, 3)
-    token_step(3)
-    token_step(4)
     query_step(0, 4)
-    token_step(5)
     output_step(0, 1)
+    token_close()
     project(0, y + ny - 3, ny - 1)
     query_step(0, 5)
     project(0, y + 4, 1)
     heads(0, lambda step: output_step(0, step))
     collected = reduce(0, lambda step: query_step(1, step))
+    def gather_step(step):
+        for lane in range(4):
+            k = x_hi if lane < 2 else 1 - x_hi
+            half = x_lo if lane % 2 == 0 else 1 - x_lo
+            ring_step(
+                step,
+                lambda b: xs_two.at[b, half, k],
+                z,
+                nz,
+                z_next,
+                REACH[(lane // 2 + lane) % 2],
+                ag_ss.at[lane],
+                ag_rs.at[lane],
+                lane % 2 == 0,
+            )
+
     for lane in range(2):
         k = x_hi if lane == 0 else 1 - x_hi
         xs_two[z, x_lo, k] = collected(lane)
-    ref = xs_two.at[z, x_lo]
-    send(ref, ref, one_ss.at[1], one_rs.at[1], beside)
-    for step in range(1, 6):
-        for lane in range(2):
-            half = x_lo if lane == 0 else 1 - x_lo
-            if step == 1 and lane == 1:
-                landed(xs_two.at[z, half], one_ss.at[1], one_rs.at[1])
-            ring_step(step, lambda b: xs_two.at[b, half], z, nz, z_next, REACH[lane], ag_ss.at[lane], ag_rs.at[lane])
-        if step == 1:
-            query_step(1, 5)
-            clear()
-        output_step(1, step)
-        if step == 4:
-            project(1, z + nz - 3, nz - 1)
+        ref = xs_two.at[z, x_lo, k]
+        for way in range(2):
+            send(ref, ref, ag_ss.at[2 * lane, way, 0], ag_rs.at[2 * lane, way, 0], z_next[way])
+        for way in range(2):
+            send(ref, ref, ag_ss.at[2 * lane + 1, way, 0], ag_rs.at[2 * lane + 1, way, 0], diagonal[way])
+        send(ref, ref, one_ss.at[1 + lane], one_rs.at[1 + k], beside)
+    clear()
+    gather_step(2)
+    query_step(1, 4)
+    gather_step(3)
+    output_step(1, 1)
+    gather_step(4)
+    query_step(1, 5)
+    for k in range(2):
+        landed(xs_two.at[z, 1 - x_lo, k], one_ss.at[1 + k], one_rs.at[1 + k])
+    project(1, z + nz - 3, nz - 1)
+    gather_step(5)
     project(1, z + 4, 1)
-    heads(1, nothing)
+    heads(1, lambda step: output_step(1, step))
     collected = reduce(1, nothing)
     for lane in range(2):
         k = x_hi if lane == 0 else 1 - x_hi
@@ -516,10 +603,10 @@
                 dma((nz,)),
                 dma((2, 5)),
                 dma((2, 5)),
-                dma((10, 2, 4)),
-                dma((10, 2, 4)),
-                dma((2, 4)),
-                dma((2, 4)),
+                dma((18, 2, 4)),
+                dma((18, 2, 4)),
+                dma((2, 2, 4)),
+                dma((2, 2, 4)),
                 dma((2, 2)),
                 dma((2, 2)),
                 dma((2,)),
@@ -530,10 +617,10 @@
                 dma((2, 2, 4)),
                 dma((2, 2, 2, 4)),
                 dma((2, 2, 2, 4)),
-                dma((2, 2, 4)),
-                dma((2, 2, 4)),
-                dma((2,)),
-                dma((2,)),
+                dma((4, 2, 4)),
+                dma((4, 2, 4)),
+                dma((4,)),
+                dma((4,)),
                 dma((2,)),
                 dma((2,)),
             ],

time: 132 us -> 114 us (0.86)
  Pallas kernels: 131 us -> 114 us
    pallas_call x1, Pallas kernels: 131 us -> 114 us  [shards(): pl.pallas_call(functools.partial(kernel, ny, nz), out_shape=jax.ShapeDtyp...]
where the time goes in v3:
time: 114 us
  Pallas kernels  114 us (100%)
    pallas_call x1, Pallas kernels, shards(): pl.pallas_call(functools.partial(kernel, ny, nz), out_shape=jax.ShapeDtyp...  114 us

profile of v3, /device:TPU:2, one launch (start us, length us, event | category | flops | bytes accessed | tf_op | source)
XLA Modules:
  0.0 114.3 jit_solution(8922800780404123950)
XLA Ops:
  0.0 113.6 %shard_map.82 = bf16[160,256]{1,0:T(8,128)(2,1)S(1)} custom-call(bf16[160,8192]{1,0:T(8,128)(2,1)} %tokens.1, s32[16,160]{1,0:T(8,128)} %docs.1, bf16[512,128]{1,0:T(8,128)(2,1)} %query_one.1, bf16[32,512]{1,0:T(8,128)(2,1)} %bitcast.2, bf16[128,512]{1,0:T(8,128)(2,1)} %output_one.1, bf16[512,128]{1,0:T(8,128)(2,1)} %query_two.1, bf16[32,512]{1,0:T(8,128)(2,1)} %bitcast.3, ...), custom_call_target="tpu_custom_call" | custom-call | flops 2000000000 | bytes 10000000 | tf_op jit(solution)/shard_map/pallas_call | solution.py:575
  113.6 0.6 copy.10

commit v4 on v3

--- a/solution.py
+++ b/solution.py
@@ -62,6 +62,8 @@
     swap_rs,
     y_ss,
     y_rs,
+    far_tok_ss,
+    far_tok_rs,
     tok_ss,
     tok_rs,
     near_ss,
@@ -93,6 +95,7 @@
     across = (inst + 1 - 2 * x_hi, rank)
     beside = (inst, rank + 2 - 4 * x_lo)
     y_next = (((inst + 2) % ninst, rank), ((inst + ninst - 2) % ninst, rank))
+    y_next_mate = tuple((peer, rank + 1 - 2 * c) for peer, _ in y_next)
     z_next = ((inst, (rank + 4) % nrank), (inst, (rank + nrank - 4) % nrank))
     across_beside = (inst + 1 - 2 * x_hi, rank + 2 - 4 * x_lo)
     across_beside_mate = (inst + 1 - 2 * x_hi, rank + 3 - 4 * x_lo - 2 * c)
@@ -112,7 +115,7 @@
 
     barrier = pltpu.get_barrier_semaphore()
     greeted = sharers + [other_z, other_diagonal, *z_second, *y_next, across, origins[0]]
-    greeted += [across_beside, across_beside_mate]
+    greeted += [across_beside, across_beside_mate, *y_next_mate]
     for peer in greeted:
         pl.semaphore_signal(barrier, inc=1, device_id=peer, device_id_type=MESH)
 
@@ -136,6 +139,10 @@
         move = copy(*args)
         move.start()
         sent.append(move)
+
+    def drain(kept):
+        while len(sent) > kept:
+            sent.pop(0).wait_send()
 
     def landed(dst, send_sem, recv_sem):
         copy(dst, dst, send_sem, recv_sem, mate).wait_recv()
@@ -186,111 +193,90 @@
         swap(layer, 3, outputs[layer].at[:, part(1 - x_lo, c)], dst, beside)
         swap(layer, 4, outputs[layer].at[:, part(1 - x_lo, 1 - c)], dst, beside_mate)
 
-    swap_query(0)
-    token_rows = [pl.ds(lane * (ROWS // 2), ROWS // 2) for lane in range(2)]
-    for lane, rows in enumerate(token_rows):
-        src = tokens.at[rows, quarter(z, 1 - x_hi)]
-        send(src, xs.at[z, x_hi, rows], one_ss.at[3 * lane], one_rs.at[3 * lane], across_beside)
-
-    def ring_step(step, slot, me, n, peers, reach, ss, rs, opens=True):
+    def ring_step(step, lanes, me, n, peers):
+        for slot, reach, ss, rs, opens in lanes:
+            for way in range(2):
+                block = (me + (n - 1 if way == 0 else 1) * (step - 1)) % n
+                if 1 < step <= reach[way] + 1:
+                    landed(slot(block), ss.at[way, step - 2], rs.at[way, step - 2])
+                if step <= reach[way] and (opens or step > 1):
+                    ref = slot(block)
+                    send(ref, ref, ss.at[way, step - 1], rs.at[way, step - 1], peers[way])
+
+    def query_open(layer):
         for way in range(2):
-            sign = 1 if way == 0 else n - 1
-            block = (me + (n - sign) * (step - 1)) % n
-            if 1 < step <= reach[way] + 1:
-                landed(slot(block), ss.at[way, step - 2], rs.at[way, step - 2])
-            if step <= reach[way] and (opens or step > 1):
-                ref = slot(block)
-                send(ref, ref, ss.at[way, step - 1], rs.at[way, step - 1], peers[way])
+            for keep in range(2):
+                core = c if keep == 0 else 1 - c
+                peer = y_next[way] if keep == 0 else y_next_mate[way]
+                for part in range(2):
+                    unit = 10 * layer + 2 * keep + part
+                    rows = pl.ds(pl.multiple_of(core * WIDE + part * HEAD, HEAD), HEAD)
+                    dst = wq.at[layer, y, c, pl.ds(part * HEAD, HEAD)]
+                    send(queries[layer].at[rows, :], dst, y_ss.at[unit, way, 0], y_rs.at[unit, way, 0], peer)
+                unit = 10 * layer + 4 + keep
+                src = keyvals[layer].at[:, own_k if keep == 0 else mate_k]
+                send(src, wkv.at[layer, y, c], y_ss.at[unit, way, 0], y_rs.at[unit, way, 0], peer)
 
     def query_step(layer, step):
-        if step == 1:
-            loads[f"q{layer}"].wait()
-        for lane in range(4):
-            head = c if lane < 2 else 1 - c
-            if step == 1 and lane == 2:
-                swapped(layer, 0, wq.at[layer, y, 1 - c])
-            unit = 9 * layer + lane
+        def lane_of(lane):
+            keep = lane // 2 if lane < 4 else lane - 4
+            head = c if keep == 0 else 1 - c
             rows = pl.ds(lane % 2 * HEAD, HEAD)
-            ring_step(
-                step,
-                lambda b: wq.at[layer, b, head, rows],
-                y,
-                ny,
-                y_next,
-                REACH[lane % 2],
-                y_ss.at[unit],
-                y_rs.at[unit],
-            )
-        if step == 1:
-            loads[f"kv{layer}"].wait()
-            swapped(layer, 1, wkv.at[layer, y, 1 - c])
-        unit = 9 * layer + 4
-        ring_step(step, lambda b: wkv.at[layer, b], y, ny, y_next, REACH[layer], y_ss.at[unit], y_rs.at[unit])
+
+            def slot(b):
+                return wq.at[layer, b, head, rows] if lane < 4 else wkv.at[layer, b, head]
+
+            unit = 10 * layer + lane
+            return slot, REACH[lane % 2], y_ss.at[unit], y_rs.at[unit], False
+
+        ring_step(step, [lane_of(lane) for lane in range(6)], y, ny, y_next)
+
+    def query_ready(layer):
+        loads[f"q{layer}"].wait()
+        loads[f"kv{layer}"].wait()
+        swapped(layer, 0, wq.at[layer, y, 1 - c])
+        swapped(layer, 1, wkv.at[layer, y, 1 - c])
 
     def output_step(layer, step):
+        def lane_of(lane):
+            lo = x_lo if lane < 2 else 1 - x_lo
+            core = c if lane % 2 == 0 else 1 - c
+            unit = 10 * layer + 6 + lane
+            return lambda b: wo.at[layer, b, lo, core], REACH[lane % 2], y_ss.at[unit], y_rs.at[unit], True
+
         if step == 1:
             loads[f"o{layer}"].wait()
-        for lane in range(4):
-            lo = x_lo if lane < 2 else 1 - x_lo
-            core = c if lane % 2 == 0 else 1 - c
-            if step == 1 and lane > 0:
-                swapped(layer, 1 + lane, wo.at[layer, y, lo, core])
-            unit = 9 * layer + 5 + lane
-            ring_step(
-                step,
-                lambda b: wo.at[layer, b, lo, core],
-                y,
-                ny,
-                y_next,
-                REACH[lane % 2],
-                y_ss.at[unit],
-                y_rs.at[unit],
-            )
-
-    def token_part(b, lane):
-        return xs.at[b, 1 - x_hi, token_rows[lane]]
-
-    def token_block(way, distance):
-        return (z + (nz - distance if way == 0 else distance)) % nz
-
-    def token_send(lane, way, message, b, peers):
-        ref = token_part(b, lane)
-        send(ref, ref, tok_ss.at[lane, way, message], tok_rs.at[lane, way, message], peers[way])
-
-    def token_landed(lane, way, distance):
-        n = distance - 1
-        landed(token_part(token_block(way, distance), lane), tok_ss.at[lane, way, n], tok_rs.at[lane, way, n])
+            for lane in range(1, 4):
+                lo = x_lo if lane < 2 else 1 - x_lo
+                swapped(layer, 1 + lane, wo.at[layer, y, lo, c if lane % 2 == 0 else 1 - c])
+        ring_step(step, [lane_of(lane) for lane in range(4)], y, ny, y_next)
+
+    def token_block(offset):
+        return xs.at[(z + offset) % nz, 1 - x_hi]
 
     def token_open():
-        for lane in range(2):
-            landed(token_part(z, lane), one_ss.at[3 * lane], one_rs.at[3 * lane])
-            for way in range(2):
-                token_send(lane, way, 1, z, z_second)
-            for way in range(2):
-                token_send(lane, way, 0, z, z_next)
-
-    def token_forward():
-        for lane in range(2):
-            for way in range(2):
-                token_landed(lane, way, 2)
-                b = token_block(way, 2)
-                if way == lane:
-                    token_send(lane, way, 3, b, z_second)
-                token_send(lane, way, 2, b, z_next)
+        for n, offset in enumerate((0, 2, 6, 4)):
+            b = (z + offset) % nz
+            src = tokens.at[:, quarter(b, 1 - x_hi)]
+            send(src, xs.at[b, x_hi], far_tok_ss.at[n], far_tok_rs.at[n], across_beside)
+
+    def token_forward(n, offset, ways):
+        ref = token_block(offset)
+        landed(ref, far_tok_ss.at[n], far_tok_rs.at[n])
+        for way in ways:
+            place = 0 if n == 0 else 1
+            send(ref, ref, tok_ss.at[way, place], tok_rs.at[way, place], z_next[way])
 
     def token_close():
-        for lane in range(2):
-            for way in range(2):
-                token_landed(lane, way, 1)
-                token_landed(lane, way, 3)
-                if way == lane:
-                    token_landed(lane, way, 4)
-
-    query_step(0, 1)
+        token_forward(3, 4, ())
+        for way, first, second in ((0, 7, 5), (1, 1, 3)):
+            landed(token_block(first), tok_ss.at[way, 0], tok_rs.at[way, 0])
+            landed(token_block(second), tok_ss.at[way, 1], tok_rs.at[way, 1])
+
+    query_open(0)
+    token_open()
+    swap_query(0)
     swap_output(0)
-    token_open()
-    swap_query(1)
-    swap_output(1)
 
     loads["docs"].wait()
     doc_row = jnp.broadcast_to(docs_in[pl.ds(inst, 1), :], (ROWS, ROWS)).astype(F32)
@@ -374,6 +360,7 @@
             ref = kvs.at[layer, piece]
             send(ref, ref, kv_ss.at[layer, n], kv_rs.at[layer, piece], peer)
         beside_step(4)
+        drain(20)
         for o in range(1, GROUP):
             p = (piece + o) % GROUP
             landed(kvs.at[layer, p], kv_ss.at[layer, 0], kv_rs.at[layer, p])
@@ -386,7 +373,7 @@
         probs = (weights / jnp.sum(weights, axis=1, keepdims=True)).astype(BF16)
         place = 2 * x_lo + c
         ctx[layer, x_hi, place] = dot_nt(probs, values).astype(BF16)
-        peers = (across, across_beside, across_beside_mate, beside, beside_mate, mate)
+        peers = (beside, beside_mate, across, mate, across_beside, across_beside_mate)
         spread(layer, x_hi, peers, 0)
         beside_step(5)
 
@@ -406,9 +393,13 @@
             left = jnp.concatenate([ctx[layer, k, n] for n in range(4)], axis=1)
 
             def body(j, carry):
-                b = (z + 3 + j) % nz
-                right = wo[layer, b].reshape(4 * HEAD, HEAD)
-                pbuf[b, k] = jnp.dot(left, right, preferred_element_type=F32)
+                b, b_next = (z + 3 + 2 * j) % nz, (z + 4 + 2 * j) % nz
+                right = jnp.concatenate(
+                    [wo[layer, b].reshape(4 * HEAD, HEAD), wo[layer, b_next].reshape(4 * HEAD, HEAD)], axis=1
+                )
+                both = jnp.dot(left, right, preferred_element_type=F32)
+                pbuf[b, k] = both[:, :HEAD]
+                pbuf[b_next, k] = both[:, HEAD:]
                 return carry
 
             lax.fori_loop(first, last, body, 0)
@@ -436,11 +427,11 @@
 
         def set_out(lane):
             k = ks[lane]
-            products(k, 0, 3)
+            products(k, 0, 2)
             put(lane, lane, 0, pbuf[block(lane, 4), k], z_second)
             for way in range(2):
                 put(lane, way, 1, pbuf[block(way, 3), k], z_next)
-            products(k, 3, nz)
+            products(k, 2, nz // 2)
             for way in range(2):
                 put(lane, way, 3, pbuf[block(way, 1), k], z_next)
 
@@ -454,13 +445,15 @@
         beside_step(1)
         for place in others:
             spread_in(layer, x_hi, place)
+        output_step(layer, 5)
+        set_out(0)
         spread_in(layer, 1 - x_hi, 2 * x_lo + c)
         spread(layer, 1 - x_hi, (mate,), 6)
-        set_out(0)
         for place in others:
             spread_in(layer, 1 - x_hi, place)
         set_out(1)
         beside_step(2)
+        drain(20)
         pass_on(0)
         pass_on(1)
         beside_step(3)
@@ -485,31 +478,34 @@
     for b in range(nz):
         loads[("x", b)].wait()
     query_step(0, 2)
-    token_forward()
+    token_forward(0, 0, (0, 1))
+    swap_query(1)
+    swap_output(1)
+    token_forward(1, 2, (1,))
     query_step(0, 3)
+    token_forward(2, 6, (0,))
+    output_step(0, 1)
     query_step(0, 4)
-    output_step(0, 1)
+    query_ready(0)
     token_close()
     project(0, y + ny - 3, ny - 1)
+    output_step(0, 2)
     query_step(0, 5)
     project(0, y + 4, 1)
-    heads(0, lambda step: output_step(0, step))
-    collected = reduce(0, lambda step: query_step(1, step))
+    def beside_heads(step):
+        if step in (3, 4):
+            output_step(0, step)
+
+    heads(0, beside_heads)
+    collected = reduce(0, lambda step: query_open(1) if step == 1 else query_step(1, step))
     def gather_step(step):
-        for lane in range(4):
+        def lane_of(lane):
             k = x_hi if lane < 2 else 1 - x_hi
             half = x_lo if lane % 2 == 0 else 1 - x_lo
-            ring_step(
-                step,
-                lambda b: xs_two.at[b, half, k],
-                z,
-                nz,
-                z_next,
-                REACH[(lane // 2 + lane) % 2],
-                ag_ss.at[lane],
-                ag_rs.at[lane],
-                lane % 2 == 0,
-            )
+            reach = REACH[(lane // 2 + lane) % 2]
+            return lambda b: xs_two.at[b, half, k], reach, ag_ss.at[lane], ag_rs.at[lane], lane % 2 == 0
+
+        ring_step(step, [lane_of(lane) for lane in range(4)], z, nz, z_next)
 
     for lane in range(2):
         k = x_hi if lane == 0 else 1 - x_hi
@@ -524,15 +520,15 @@
     gather_step(2)
     query_step(1, 4)
     gather_step(3)
-    output_step(1, 1)
     gather_step(4)
     query_step(1, 5)
     for k in range(2):
         landed(xs_two.at[z, 1 - x_lo, k], one_ss.at[1 + k], one_rs.at[1 + k])
+    query_ready(1)
     project(1, z + nz - 3, nz - 1)
     gather_step(5)
     project(1, z + 4, 1)
-    heads(1, lambda step: output_step(1, step))
+    heads(1, lambda step: output_step(1, step - 1))
     collected = reduce(1, nothing)
     for lane in range(2):
         k = x_hi if lane == 0 else 1 - x_hi
@@ -555,8 +551,7 @@
         keep.wait()
 
     moves[1].wait_send()
-    for move in sent:
-        move.wait_send()
+    drain(0)
     landed(out.at[:, :HEAD], fin_ss.at[0], fin_rs.at[0])
 
     @pl.when(stays == 0)
@@ -603,10 +598,12 @@
                 dma((nz,)),
                 dma((2, 5)),
                 dma((2, 5)),
-                dma((18, 2, 4)),
-                dma((18, 2, 4)),
-                dma((2, 2, 4)),
-                dma((2, 2, 4)),
+                dma((20, 2, 4)),
+                dma((20, 2, 4)),
+                dma((4,)),
+                dma((4,)),
+                dma((2, 2)),
+                dma((2, 2)),
                 dma((2, 2)),
                 dma((2, 2)),
                 dma((2,)),

time: 114 us -> 111 us (0.974)
  Pallas kernels: 114 us -> 110 us
    pallas_call x1, Pallas kernels: 114 us -> 110 us  [shards(): pl.pallas_call(functools.partial(kernel, ny, nz), out_shape=jax.ShapeDtyp...]
where the time goes in v4:
time: 111 us
  Pallas kernels  110 us (99%)
    pallas_call x1, Pallas kernels, shards(): pl.pallas_call(functools.partial(kernel, ny, nz), out_shape=jax.ShapeDtyp...  110 us

profile of v4, /device:TPU:2, one launch (start us, length us, event | category | flops | bytes accessed | tf_op | source)
XLA Modules:
  0.0 110.6 jit_solution(14962370079789614972)
XLA Ops:
  0.0 110.0 %shard_map.82 = bf16[160,256]{1,0:T(8,128)(2,1)S(1)} custom-call(bf16[160,8192]{1,0:T(8,128)(2,1)} %tokens.1, s32[16,160]{1,0:T(8,128)} %docs.1, bf16[512,128]{1,0:T(8,128)(2,1)} %query_one.1, bf16[32,512]{1,0:T(8,128)(2,1)} %bitcast.2, bf16[128,512]{1,0:T(8,128)(2,1)} %output_one.1, bf16[512,128]{1,0:T(8,128)(2,1)} %query_two.1, bf16[32,512]{1,0:T(8,128)(2,1)} %bitcast.3, ...), custom_call_target="tpu_custom_call" | custom-call | flops 2000000000 | bytes 10000000 | tf_op jit(solution)/shard_map/pallas_call | solution.py:570
  110.0 0.6 copy.10

commit v5 on v4

--- a/solution.py
+++ b/solution.py
@@ -41,6 +41,7 @@
     docs_in,
     mask,
     xs,
+    xs_own,
     xs_two,
     aq,
     akv,
@@ -57,6 +58,7 @@
     rs_r,
     fin,
     local_sem,
+    own_sem,
     xlocal_sem,
     swap_ss,
     swap_rs,
@@ -64,6 +66,8 @@
     y_rs,
     far_tok_ss,
     far_tok_rs,
+    mate_tok_ss,
+    mate_tok_rs,
     tok_ss,
     tok_rs,
     near_ss,
@@ -100,7 +104,6 @@
     across_beside = (inst + 1 - 2 * x_hi, rank + 2 - 4 * x_lo)
     across_beside_mate = (inst + 1 - 2 * x_hi, rank + 3 - 4 * x_lo - 2 * c)
     beside_mate = (inst, rank + 3 - 4 * x_lo - 2 * c)
-    goals = [((2 * y + k + 1) % ninst, 4 * z + 2 * x_hi + c) for k in range(2)]
     origin_inst = (inst + ninst - 1) % ninst // 2 * 2 + x_lo
     origins = [(origin_inst, 4 * z + 2 * s + c) for s in range(2)]
     stays = x_hi * x_lo
@@ -114,8 +117,8 @@
     diagonal = tuple((inst, peer + 2 - 4 * x_lo) for _, peer in z_next)
 
     barrier = pltpu.get_barrier_semaphore()
-    greeted = sharers + [other_z, other_diagonal, *z_second, *y_next, across, origins[0]]
-    greeted += [across_beside, across_beside_mate, *y_next_mate]
+    greeted = [*y_next, across_beside, *y_next_mate, *sharers, other_z, other_diagonal, *z_second]
+    greeted += [across, across_beside_mate, origins[0]]
     for peer in greeted:
         pl.semaphore_signal(barrier, inc=1, device_id=peer, device_id_type=MESH)
 
@@ -161,17 +164,7 @@
 
     own_k = pl.ds(pl.multiple_of(c * WIDE, WIDE), WIDE)
     mate_k = pl.ds(pl.multiple_of((1 - c) * WIDE, WIDE), WIDE)
-    own_part = pl.ds(pl.multiple_of((2 * c + x_lo) * HEAD, HEAD), HEAD)
-    load("kv0", keyvals[0].at[:, own_k], wkv.at[0, y, c], local_sem.at[0])
-    load("q0", queries[0].at[own_k, :], wq.at[0, y, c], local_sem.at[1])
-    for b in range(nz):
-        load(("x", b), tokens.at[:, quarter(b, x_hi)], xs.at[b, x_hi], xlocal_sem.at[b])
-    load("o0", outputs[0].at[:, own_part], wo.at[0, y, x_lo, c], local_sem.at[2])
-    load("docs", docs, docs_in, local_sem.at[3])
-    load("kv1", keyvals[1].at[:, own_k], wkv.at[1, y, c], local_sem.at[4])
-    load("q1", queries[1].at[own_k, :], wq.at[1, y, c], local_sem.at[5])
-    load("o1", outputs[1].at[:, own_part], wo.at[1, y, x_lo, c], local_sem.at[6])
-
+    halves = [pl.ds(half * WIDE, WIDE) for half in range(2)]
     pl.semaphore_wait(barrier, len(greeted) + 1 - stays)
 
     def swap(layer, n, src, dst, peer):
@@ -205,6 +198,17 @@
 
     def query_open(layer):
         for way in range(2):
+            if layer == 0:
+                for half in range(2):
+                    for part in range(2):
+                        unit = 2 * half + part
+                        rows = pl.ds(half * WIDE + part * HEAD, HEAD)
+                        dst = wq.at[0, y, half, pl.ds(part * HEAD, HEAD)]
+                        send(queries[0].at[rows, :], dst, y_ss.at[unit, way, 0], y_rs.at[unit, way, 0], y_next[way])
+                    src = keyvals[0].at[:, halves[half]]
+                    unit = 4 + half
+                    send(src, wkv.at[0, y, half], y_ss.at[unit, way, 0], y_rs.at[unit, way, 0], y_next[way])
+                continue
             for keep in range(2):
                 core = c if keep == 0 else 1 - c
                 peer = y_next[way] if keep == 0 else y_next_mate[way]
@@ -220,7 +224,7 @@
     def query_step(layer, step):
         def lane_of(lane):
             keep = lane // 2 if lane < 4 else lane - 4
-            head = c if keep == 0 else 1 - c
+            head = keep if layer == 0 else c if keep == 0 else 1 - c
             rows = pl.ds(lane % 2 * HEAD, HEAD)
 
             def slot(b):
@@ -232,6 +236,11 @@
         ring_step(step, [lane_of(lane) for lane in range(6)], y, ny, y_next)
 
     def query_ready(layer):
+        if layer == 0:
+            for half in range(2):
+                loads["q0", half].wait()
+                loads["kv0", half].wait()
+            return
         loads[f"q{layer}"].wait()
         loads[f"kv{layer}"].wait()
         swapped(layer, 0, wq.at[layer, y, 1 - c])
@@ -252,13 +261,13 @@
         ring_step(step, [lane_of(lane) for lane in range(4)], y, ny, y_next)
 
     def token_block(offset):
-        return xs.at[(z + offset) % nz, 1 - x_hi]
+        return xs.at[(z + offset) % nz, c]
 
     def token_open():
         for n, offset in enumerate((0, 2, 6, 4)):
             b = (z + offset) % nz
             src = tokens.at[:, quarter(b, 1 - x_hi)]
-            send(src, xs.at[b, x_hi], far_tok_ss.at[n], far_tok_rs.at[n], across_beside)
+            send(src, xs.at[b, c], far_tok_ss.at[n], far_tok_rs.at[n], across_beside)
 
     def token_forward(n, offset, ways):
         ref = token_block(offset)
@@ -266,17 +275,41 @@
         for way in ways:
             place = 0 if n == 0 else 1
             send(ref, ref, tok_ss.at[way, place], tok_rs.at[way, place], z_next[way])
+        token_share(offset)
+
+    def token_share(offset):
+        ref = token_block(offset)
+        send(ref, ref, mate_tok_ss.at[offset], mate_tok_rs.at[offset], mate)
 
     def token_close():
         token_forward(3, 4, ())
         for way, first, second in ((0, 7, 5), (1, 1, 3)):
             landed(token_block(first), tok_ss.at[way, 0], tok_rs.at[way, 0])
+            token_share(first)
             landed(token_block(second), tok_ss.at[way, 1], tok_rs.at[way, 1])
+            token_share(second)
+
+    def token_finish():
+        for offset in range(nz):
+            landed(xs.at[(z + offset) % nz, 1 - c], mate_tok_ss.at[offset], mate_tok_rs.at[offset])
 
     query_open(0)
     token_open()
-    swap_query(0)
+    own_part = pl.ds(pl.multiple_of((2 * c + x_lo) * HEAD, HEAD), HEAD)
+    for half in range(2):
+        load(("kv0", half), keyvals[0].at[:, halves[half]], wkv.at[0, y, half], own_sem.at[half])
+        load(("q0", half), queries[0].at[halves[half], :], wq.at[0, y, half], own_sem.at[2 + half])
+    for b in range(nz):
+        columns = pl.ds(pl.multiple_of((2 * b + x_hi) * 512, 512), 512)
+        load(("x", b), tokens.at[:, columns], xs_own.at[b], xlocal_sem.at[b])
+    load("o0", outputs[0].at[:, own_part], wo.at[0, y, x_lo, c], local_sem.at[2])
+    load("docs", docs, docs_in, local_sem.at[3])
+    load("kv1", keyvals[1].at[:, own_k], wkv.at[1, y, c], local_sem.at[4])
+    load("q1", queries[1].at[own_k, :], wq.at[1, y, c], local_sem.at[5])
+    load("o1", outputs[1].at[:, own_part], wo.at[1, y, x_lo, c], local_sem.at[6])
     swap_output(0)
+
+    token_forward(0, 0, (0, 1))
 
     loads["docs"].wait()
     doc_row = jnp.broadcast_to(docs_in[pl.ds(inst, 1), :], (ROWS, ROWS)).astype(F32)
@@ -310,13 +343,26 @@
         akv[...] = jnp.zeros_like(akv)
         ass[...] = jnp.zeros_like(ass)
 
+    def project_one(own, first, count):
+        k = x_hi if own else 1 - x_hi
+
+        def body(j, carry):
+            b = (first + j) % nz
+            x = xs_own[b] if own else jnp.concatenate([xs[b, 0], xs[b, 1]], axis=1)
+            xf = x.astype(F32)
+            sq = xf * xf
+            ass[k] += sq[:, :HEAD] + sq[:, HEAD:WIDE] + sq[:, WIDE : WIDE + HEAD] + sq[:, WIDE + HEAD :]
+            aq[c, k] += jnp.dot(x, wq[0, b].reshape(2 * WIDE, HEAD), preferred_element_type=F32)
+            turned = jnp.concatenate([wkv[0, b, 0], wkv[0, b, 1]], axis=1)
+            akv[c, k, :, :PIECE] += dot_nt(x, turned)
+            return carry
+
+        lax.fori_loop(0, count, body, 0)
+
     def project(layer, first, count):
         def body(j, carry):
             b = (first + j) % nz
-            if layer == 0:
-                x = xs[b].reshape(2 * ROWS, WIDE)
-            else:
-                x = jnp.concatenate([xs_two[b, 0].reshape(2 * ROWS, HEAD), xs_two[b, 1].reshape(2 * ROWS, HEAD)], axis=1)
+            x = jnp.concatenate([xs_two[b, 0].reshape(2 * ROWS, HEAD), xs_two[b, 1].reshape(2 * ROWS, HEAD)], axis=1)
             w = jnp.concatenate([wq[layer, b, 0], wq[layer, b, 1]], axis=1)
             q = jnp.dot(x, w, preferred_element_type=F32).reshape(2, ROWS, WIDE)
             xf = x.astype(F32)
@@ -330,23 +376,26 @@
         lax.fori_loop(0, count, body, 0)
 
     def heads(layer, beside_step):
-        for k in (1 - x_hi, x_hi):
+        for k in (1 - x_hi, x_hi) if layer == 1 else ():
             squares = jnp.sum(ass[k], axis=1, keepdims=True)
             pack(near_s.at[layer, k], aq[1 - c, k], akv[1 - c, k], squares)
             send(near_s.at[layer, k], near_r.at[layer, k], near_ss.at[layer, k], near_rs.at[layer, k], mate)
         beside_step(2)
 
         def chip_sum(k):
+            squares = jnp.sum(ass[k], axis=1, keepdims=True)
+            tail = jnp.where(lane_at < PIECE, akv[c, k], jnp.where(lane_at == PIECE, squares, 0.0))
+            if layer == 0:
+                return aq[c, k], tail
             landed(near_r.at[layer, k], near_ss.at[layer, k], near_rs.at[layer, k])
-            squares = jnp.sum(ass[k], axis=1, keepdims=True)
             other = near_r[layer, k].astype(F32)
-            tail = jnp.where(lane_at < PIECE, akv[c, k], jnp.where(lane_at == PIECE, squares, 0.0))
             return aq[c, k] + other[:, :HEAD], tail + other[:, HEAD:]
 
         q, tail = chip_sum(1 - x_hi)
         pack(far_s.at[layer], q, tail, squares_of(tail))
         send(far_s.at[layer], far_r.at[layer], far_ss.at[layer], far_rs.at[layer], across)
         beside_step(3)
+        drain(30)
         q, tail = chip_sum(x_hi)
         landed(far_r.at[layer], far_ss.at[layer], far_rs.at[layer])
         other = far_r[layer].astype(F32)
@@ -360,7 +409,6 @@
             ref = kvs.at[layer, piece]
             send(ref, ref, kv_ss.at[layer, n], kv_rs.at[layer, piece], peer)
         beside_step(4)
-        drain(20)
         for o in range(1, GROUP):
             p = (piece + o) % GROUP
             landed(kvs.at[layer, p], kv_ss.at[layer, 0], kv_rs.at[layer, p])
@@ -453,10 +501,10 @@
             spread_in(layer, 1 - x_hi, place)
         set_out(1)
         beside_step(2)
-        drain(20)
         pass_on(0)
         pass_on(1)
         beside_step(3)
+        drain(30)
 
         def collected(lane):
             total = pbuf[z, ks[lane]]
@@ -464,7 +512,10 @@
                 total = total + got(lane, way, 3) + got(lane, way, 2)
             k = ks[lane]
             if layer == 0:
-                old = xs[z, k, :, pl.ds(pl.multiple_of(x_lo * HEAD, HEAD), HEAD)]
+                if lane == 0:
+                    old = xs_own[z, :, pl.ds(pl.multiple_of(c * WIDE + x_lo * HEAD, HEAD), HEAD)]
+                else:
+                    old = xs[z, c, :, pl.ds(pl.multiple_of(x_lo * HEAD, HEAD), HEAD)]
             else:
                 old = xs_two[z, x_lo, k]
             return (old.astype(F32) + total).astype(BF16)
@@ -478,20 +529,25 @@
     for b in range(nz):
         loads[("x", b)].wait()
     query_step(0, 2)
-    token_forward(0, 0, (0, 1))
+    token_forward(1, 2, (1,))
+    token_forward(2, 6, (0,))
     swap_query(1)
     swap_output(1)
-    token_forward(1, 2, (1,))
     query_step(0, 3)
-    token_forward(2, 6, (0,))
     output_step(0, 1)
+    query_ready(0)
+    project_one(True, y + ny - 2, 5)
+    token_close()
     query_step(0, 4)
-    query_ready(0)
-    token_close()
-    project(0, y + ny - 3, ny - 1)
+    token_finish()
+    project_one(True, y + 3, 1)
+    project_one(True, y + ny - 3, 1)
+    project_one(False, y + ny - 3, ny - 1)
     output_step(0, 2)
     query_step(0, 5)
-    project(0, y + 4, 1)
+    project_one(False, y + 4, 1)
+    project_one(True, y + 4, 1)
+
     def beside_heads(step):
         if step in (3, 4):
             output_step(0, step)
@@ -530,27 +586,29 @@
     project(1, z + 4, 1)
     heads(1, lambda step: output_step(1, step - 1))
     collected = reduce(1, nothing)
-    for lane in range(2):
+    own_half = pl.ds(pl.multiple_of(x_lo * HEAD, HEAD), HEAD)
+
+    def deliver(lane):
         k = x_hi if lane == 0 else 1 - x_hi
-        fin[k] = collected(lane)
-    own_half = pl.ds(pl.multiple_of(x_lo * HEAD, HEAD), HEAD)
-    moves = [
-        copy(fin.at[k], out.at[:, own_half], fin_ss.at[k], fin_rs.at[x_lo], goals[k]) for k in range(2)
-    ]
-    moves[1].start()
+        goal = ((2 * y + k + 1) % ninst, 4 * z + 2 * x_hi + c)
+        return copy(fin.at[lane], out.at[:, own_half], fin_ss.at[lane], fin_rs.at[x_lo], goal)
+
+    fin[0] = collected(0)
+    deliver(0).start()
+    fin[1] = collected(1)
 
     @pl.when(stays == 0)
     def _():
-        moves[0].start()
-        moves[0].wait_send()
+        deliver(1).start()
+        deliver(1).wait_send()
 
     @pl.when(stays == 1)
     def _():
-        keep = pltpu.make_async_copy(fin.at[0], out.at[:, own_half], local_sem.at[0])
+        keep = pltpu.make_async_copy(fin.at[1], out.at[:, own_half], local_sem.at[0])
         keep.start()
         keep.wait()
 
-    moves[1].wait_send()
+    deliver(0).wait_send()
     drain(0)
     landed(out.at[:, :HEAD], fin_ss.at[0], fin_rs.at[0])
 
@@ -579,6 +637,7 @@
                 vmem((2 * ny, ROWS), jnp.int32),
                 vmem((ROWS, WIDE), F32),
                 vmem((nz, 2, ROWS, WIDE), BF16),
+                vmem((nz, ROWS, 2 * WIDE), BF16),
                 vmem((nz, 2, 2, ROWS, HEAD), BF16),
                 vmem((2, 2, ROWS, HEAD), F32),
                 vmem((2, 2, ROWS, HEAD), F32),
@@ -595,6 +654,7 @@
                 vmem((2, 2, 2, 4, ROWS, HEAD), BF16),
                 vmem((2, ROWS, HEAD), BF16),
                 dma((7,)),
+                dma((4,)),
                 dma((nz,)),
                 dma((2, 5)),
                 dma((2, 5)),
@@ -602,6 +662,8 @@
                 dma((20, 2, 4)),
                 dma((4,)),
                 dma((4,)),
+                dma((nz,)),
+                dma((nz,)),
                 dma((2, 2)),
                 dma((2, 2)),
                 dma((2, 2)),

time: 111 us -> 110 us (level)
  the two profiles are of different devices: /device:TPU:2 before, /device:TPU:64 now
where the time goes in v5:
time: 110 us
  Pallas kernels  109 us (99%)
    pallas_call x1, Pallas kernels, shards(): pl.pallas_call(functools.partial(kernel, ny, nz), out_shape=jax.ShapeDtyp...  109 us

profile of v5, /device:TPU:64, one launch (start us, length us, event | category | flops | bytes accessed | tf_op | source)
XLA Modules:
  0.0 110.1 jit_solution(9844735303419666911)
XLA Ops:
  0.0 109.5 %shard_map.82 = bf16[160,256]{1,0:T(8,128)(2,1)S(1)} custom-call(bf16[160,8192]{1,0:T(8,128)(2,1)} %tokens.1, s32[16,160]{1,0:T(8,128)} %docs.1, bf16[512,128]{1,0:T(8,128)(2,1)} %query_one.1, bf16[32,512]{1,0:T(8,128)(2,1)} %bitcast.2, bf16[128,512]{1,0:T(8,128)(2,1)} %output_one.1, bf16[512,128]{1,0:T(8,128)(2,1)} %query_two.1, bf16[32,512]{1,0:T(8,128)(2,1)} %bitcast.3, ...), custom_call_target="tpu_custom_call" | custom-call | flops 2000000000 | bytes 10000000 | tf_op jit(solution)/shard_map/pallas_call | solution.py:628
  109.5 0.6 copy.10

commit v6 on v5

--- a/solution.py
+++ b/solution.py
@@ -405,7 +405,7 @@
         q = (q * scale * HEAD**-0.5).astype(BF16)
         tail_pad[:ROWS, :] = jnp.where(lane_at < PIECE, tail * scale, 0.0).astype(BF16)
         kvs[layer, piece] = dot_nt(select, tail_pad[...]).astype(BF16)
-        for n, peer in enumerate(sharers):
+        for n, peer in enumerate(sharers[2:6] + sharers[:2] + sharers[6:]):
             ref = kvs.at[layer, piece]
             send(ref, ref, kv_ss.at[layer, n], kv_rs.at[layer, piece], peer)
         beside_step(4)

time: 110 us -> 110 us (level)
  the two profiles are of different devices: /device:TPU:64 before, /device:TPU:2 now
where the time goes in v6:
time: 110 us
  Pallas kernels  109 us (99%)
    pallas_call x1, Pallas kernels, shards(): pl.pallas_call(functools.partial(kernel, ny, nz), out_shape=jax.ShapeDtyp...  109 us

profile of v6, /device:TPU:2, one launch (start us, length us, event | category | flops | bytes accessed | tf_op | source)
XLA Modules:
  0.0 109.7 jit_solution(11215367229555419629)
XLA Ops:
  0.0 109.1 %shard_map.82 = bf16[160,256]{1,0:T(8,128)(2,1)S(1)} custom-call(bf16[160,8192]{1,0:T(8,128)(2,1)} %tokens.1, s32[16,160]{1,0:T(8,128)} %docs.1, bf16[512,128]{1,0:T(8,128)(2,1)} %query_one.1, bf16[32,512]{1,0:T(8,128)(2,1)} %bitcast.2, bf16[128,512]{1,0:T(8,128)(2,1)} %output_one.1, bf16[512,128]{1,0:T(8,128)(2,1)} %query_two.1, bf16[32,512]{1,0:T(8,128)(2,1)} %bitcast.3, ...), custom_call_target="tpu_custom_call" | custom-call | flops 2000000000 | bytes 10000000 | tf_op jit(solution)/shard_map/pallas_call | solution.py:628
  109.1 0.6 copy.10
